TPU v7x, 512 devices: a whole 4x4x16 slice. The times are simulated.
512 devices in a mesh: rows: 64 (over z, x), grp: 8 (over y, core).
Axes of the slice: x: 4, y: 4, z: 16, core: 2. Of those that a mesh axis runs over, the one named last changes fastest.
Arguments:
- panel: bfloat16 [131072, 256], P(('rows', 'grp')), may hold values from -6 to 6
- tile_lists: int32 [3, 32768], P(None, ('rows', 'grp')), may hold values from 0 to 15, as said below
- tile_values: float32 [32768, 128, 128], P(('rows', 'grp')), may hold values from -0.0625 to 0.0625
Outputs:
- basis: float32 [131072, 256], P(('rows', 'grp'))
Inputs may be any that keep to these rules, and one draw needn't show every extreme that they name: `tile_lists`: A slot facing row group s on a device of row group r is live only if s >= r; the slot with s = r is always live, and its column block is not before its row block. Row entries lie below 2; flags are 0 or 1.
All inputs are finite; a program needn't handle non-finite values.
Results may differ from a plain program's by a relative error of at most 0.0003.
Values may be sent and summed in bfloat16 or wider, within the bound.
A program may use at most 128 MiB of HBM per device.

v0:
```python
import jax
import jax.numpy as jnp
from jax import lax
from jax.sharding import PartitionSpec as P


def shards(panel, tile_lists, tile_values):
    tile = tile_values.shape[1]
    width = panel.shape[1]
    rows_here = panel.shape[0]
    blocks = rows_here // tile
    groups = lax.axis_size("grp")
    nodes = rows_here * lax.axis_size("rows") * groups
    span = groups * blocks
    highest = lax.Precision.HIGHEST
    row_local = tile_lists[0]
    col_local = tile_lists[1]
    live = tile_lists[2].astype(jnp.float32)
    masked = tile_values * live[:, None, None]
    row_pick = (row_local[:, None] == jnp.arange(blocks, dtype=jnp.int32)[None, :]).astype(
        jnp.bfloat16
    )
    own_blocks = panel.reshape(blocks, tile, width)
    row_blocks = jnp.einsum(
        "sb,btk->stk", row_pick, own_blocks, preferred_element_type=jnp.float32
    ).astype(jnp.bfloat16)
    whole = lax.all_gather(panel, "grp", axis=0, tiled=True).reshape(span, tile, width)
    span_ids = jnp.arange(span, dtype=jnp.float32)
    asked = lax.all_to_all(col_local, "rows", split_axis=0, concat_axis=0, tiled=True)
    wanted = asked.astype(jnp.float32)
    picker = (wanted[:, None] == span_ids[None, :]).astype(jnp.bfloat16)
    fetched = lax.all_to_all(
        jnp.einsum("sc,ctk->stk", picker, whole, preferred_element_type=jnp.float32).astype(
            jnp.bfloat16
        ),
        "rows",
        split_axis=0,
        concat_axis=0,
        tiled=True,
    )
    flipped = jnp.einsum("sji,sjk->sik", masked, row_blocks.astype(jnp.float32), precision=highest)
    returned = lax.all_to_all(flipped, "rows", split_axis=0, concat_axis=0, tiled=True)
    forward = jnp.einsum("sij,sjk->sik", masked, fetched.astype(jnp.float32), precision=highest)
    local_rows = jnp.einsum("sb,sik->bik", row_pick.astype(jnp.float32), forward, precision=highest)
    col_pick = (wanted[:, None] == span_ids[None, :]).astype(jnp.float32)
    spread = jnp.einsum("sc,sik->cik", col_pick, returned, precision=highest).reshape(
        span * tile, width
    )
    mine = lax.psum_scatter(spread, "grp", scatter_dimension=0, tiled=True)
    product = local_rows.reshape(rows_here, width) + mine
    partial_gram = jnp.dot(product.T, product, precision=highest)
    gram = lax.psum(partial_gram, ("rows", "grp")) / nodes
    lower = jnp.linalg.cholesky(gram)
    solved = jax.scipy.linalg.solve_triangular(lower, product.T, lower=True)
    return solved.T


def solution(mesh):
    return jax.shard_map(
        shards,
        mesh=mesh,
        in_specs=(
            P(("rows", "grp"), None),
            P(None, ("rows", "grp")),
            P(("rows", "grp"), None, None),
        ),
        out_specs=P(("rows", "grp"), None),
        check_vma=False,
    )
```

profile of v0, /device:TPU:1, one launch (start us, length us, event | category | flops | bytes accessed | tf_op | source)
XLA Modules:
  0.0 1156.1 jit_solution(11568768059573521881)
XLA Ops:
  8.0 19.1 %all-to-all-start = ((s32[64,1,1]{2,1,0:T(1,128)}), s32[64,1,1]{2,1,0:T(1,128)S(1)}, u32[]{:S(2)}, u32[]{:S(2)}) async-start(s32[64,1,1]{2,1,0:T(1,128)} %copy.41), calls=%async_computation | async-start | bytes 65536 | tf_op jit(solution)/shard_map/all_to_all | solution.py:29
  27.2 2.4 convolution_convert_fusion
  29.5 11.0 fusion.4
  40.6 14.8 %all-to-all-start.2 = ((f32[64,128,256]{2,1,0:T(8,128)}), f32[64,128,256]{2,1,0:T(8,128)}, u32[]{:S(2)}, u32[]{:S(2)}) async-start(f32[64,128,256]{2,1,0:T(8,128)} %fusion.4), calls=%async_computation.2 | async-start | bytes 16777216 | tf_op jit(solution)/shard_map/all_to_all | solution.py:42
  56.7 35.0 %all-gather.2.cloned.1.call-done = bf16[2048,256]{1,0:T(8,128)(2,1)} async-done(((bf16[256,256]{1,0:T(8,128)(2,1)}), bf16[2048,256]{1,0:T(8,128)(2,1)}) %all-gather.2.cloned.1.call-update) | async-done | bytes 1048592 | tf_op jit(solution)/shard_map/all_gather | solution.py:27
  91.6 2.5 convolution_convert_fusion.1
  94.2 4.4 copy.43
  98.5 317.8 %all-to-all-done.2 = f32[64,128,256]{2,1,0:T(8,128)} async-done(((f32[64,128,256]{2,1,0:T(8,128)}), f32[64,128,256]{2,1,0:T(8,128)}, u32[]{:S(2)}, u32[]{:S(2)}) %all-to-all-start.2) | async-done | bytes 8388640 | tf_op jit(solution)/shard_map/all_to_all | solution.py:42
  416.3 14.4 %all-to-all-start.1 = ((bf16[64,128,256]{2,1,0:T(8,128)(2,1)}), bf16[64,128,256]{2,1,0:T(8,128)(2,1)}, u32[]{:S(2)}, u32[]{:S(2)}) async-start(bf16[64,128,256]{2,1,0:T(8,128)(2,1)} %copy.43), calls=%async_computation.1 | async-start | bytes 8388608 | tf_op jit(solution)/shard_map/all_to_all | solution.py:32
  430.8 10.7 fusion
  441.5 1.2 copy.50
  442.7 1.8 copy.51
  444.8 169.6 %all-to-all-done.1 = bf16[64,128,256]{2,1,0:T(8,128)(2,1)} async-done(((bf16[64,128,256]{2,1,0:T(8,128)(2,1)}), bf16[64,128,256]{2,1,0:T(8,128)(2,1)}, u32[]{:S(2)}, u32[]{:S(2)}) %all-to-all-start.1) | async-done | bytes 4194336 | tf_op jit(solution)/shard_map/all_to_all | solution.py:32
  614.4 7.4 fusion.7
  621.8 7.5 fusion.2
  629.5 2.1 fusion.16
  632.9 452.7 %all-reduce.3.cloned.1.call-done = f32[256,256]{0,1:T(8,128)} async-done(((f32[256,256]{0,1:T(8,128)}), f32[256,256]{0,1:T(8,128)}) %all-reduce.3.cloned.1.call-update) | async-done | bytes 262160 | tf_op jit(solution)/shard_map/psum | solution.py:52
  1087.7 11.7 %cholesky.50 = f32[128,128]{1,0:T(8,128)S(1)} custom-call(f32[128,128]{1,0:T(8,128)S(1)} %cholesky.118), custom_call_target="Cholesky" | custom-call | tf_op jit(solution)/shard_map/jit(cholesky)/cholesky | solution.py:53
  1099.4 9.8 custom-call.15
  1109.7 11.7 %cholesky.105 = f32[128,128]{1,0:T(8,128)S(1)} custom-call(f32[128,128]{1,0:T(8,128)S(1)} %convolution_subtract_fusion.1), custom_call_target="Cholesky" | custom-call | tf_op jit(solution)/shard_map/jit(cholesky)/cholesky | solution.py:53
  1123.6 4.2 while.1
  1124.4 1.4 bitcast_dynamic-update-slice_fusion.2
  1126.4 1.4 bitcast_dynamic-update-slice_fusion.2
  1127.8 19.7 %custom-call.16 = f32[2,128,128]{1,2,0:T(8,128)S(1)} custom-call(f32[2,128,128]{2,1,0:T(8,128)S(1)} %get-tuple-element.12), custom_call_target="InvertDiagBlocksLowerTriangular" | custom-call | tf_op jit(solution)/shard_map/jit(_solve_triangular)/triangular_solve | solution.py:54
  (39 shorter events, 10.8 us)
Async XLA Ops:
  8.0 32.5 %all-to-all-start = ((s32[64,1,1]{2,1,0:T(1,128)}), s32[64,1,1]{2,1,0:T(1,128)S(1)}, u32[]{:S(2)}, u32[]{:S(2)}) async-start(s32[64,1,1]{2,1,0:T(1,128)} %copy.41), calls=%async_computation | async-start | bytes 65536 | tf_op jit(solution)/shard_map/all_to_all | solution.py:29
  27.2 2.4 copy-start
  40.6 375.8 %all-to-all-start.2 = ((f32[64,128,256]{2,1,0:T(8,128)}), f32[64,128,256]{2,1,0:T(8,128)}, u32[]{:S(2)}, u32[]{:S(2)}) async-start(f32[64,128,256]{2,1,0:T(8,128)} %fusion.4), calls=%async_computation.2 | async-start | bytes 16777216 | tf_op jit(solution)/shard_map/all_to_all | solution.py:42
  55.4 36.3 %all-gather.2.cloned.1.call-start = ((), (), s32[]{:S(2)}) async-start(), calls=%async_computation.4 | async-start | bytes 1179648 | tf_op jit(solution)/shard_map/all_gather | solution.py:27
  416.3 198.1 %all-to-all-start.1 = ((bf16[64,128,256]{2,1,0:T(8,128)(2,1)}), bf16[64,128,256]{2,1,0:T(8,128)(2,1)}, u32[]{:S(2)}, u32[]{:S(2)}) async-start(bf16[64,128,256]{2,1,0:T(8,128)(2,1)} %copy.43), calls=%async_computation.1 | async-start | bytes 8388608 | tf_op jit(solution)/shard_map/all_to_all | solution.py:32
  430.7 198.7 %reduce-scatter.2.cloned.1.call-start = ((), (), s32[]{:S(2)}) async-start(), calls=%async_computation.5 | async-start | bytes 2359296 | tf_op jit(solution)/shard_map/reduce_scatter | solution.py:49
  444.6 641.0 %all-reduce.3.cloned.1.call-start = ((), (), s32[]{:S(2)}) async-start(), calls=%async_computation.6 | async-start | bytes 524288 | tf_op jit(solution)/shard_map/psum | solution.py:52
Sparse Core Ops, SparseCore 0:
  58.4 33.2 all-gather.1
  444.7 42.0 reduce-scatter.1
  631.8 453.7 all-reduce.2
where the time goes:
time: 1160 us
  waiting for transfers between devices  975 us (84%)
  other arithmetic  58.2 us (5%)
  starting transfers between devices  49.1 us (4%)
  matrix products  45 us (4%)
  between operations  14.9 us (1%)
  local copies, waits for them, and re-layouts  13.2 us (1%)
    psum x1, waiting for transfers between devices, shards(): gram = lax.psum(partial_gram, ('rows', 'grp')) / nodes  453 us
    all_to_all x1, waiting for transfers between devices, shards(): lax.all_to_all(flipped, 'rows', split_axis=0, concat_axis=0, tiled=True)  318 us
    all_to_all x1, waiting for transfers between devices, shards(): lax.all_to_all(jnp.einsum('sc,ctk->stk', picker, whole, preferred_element...  170 us
    all_gather x1, waiting for transfers between devices, shards(): lax.all_gather(panel, 'grp', axis=0, tiled=True).reshape(span, tile, width)  35 us
    another operation x6, other arithmetic, shards(): lower = jnp.linalg.cholesky(gram)  34 us
  transfers between devices with their start and end apart: 6, of which 4 were waited for; matrix products, arithmetic and copies ran while one was open for 4% of the time, Pallas kernels for 0%

commit v1 on v0

v1 whole, which is shorter than its diff:
```python
import functools

import jax
import jax.numpy as jnp
from jax import lax
from jax.experimental import pallas as pl
from jax.experimental.pallas import tpu as pltpu
from jax.sharding import Mesh, PartitionSpec as P

HIGHEST = lax.Precision.HIGHEST
MESH = pl.DeviceIdType.MESH
VMEM_LIMIT = 56 * 1024 * 1024
AXES = ("z", "x", "y", "core")
PLANE = ("x", "y", "core")
GROUP = ("y", "core")


def axis_sizes():
    return tuple(lax.axis_size(a) for a in AXES)


def split2(t):
    high = t.astype(jnp.bfloat16)
    low = (t - high.astype(jnp.float32)).astype(jnp.bfloat16)
    return high, low


def tiles_kernel(his, blocks, span, step, meta, tiles, cols, rows, fwd, bwd):
    at = pl.program_id(0)

    @pl.when(at == 0)
    def _():
        bwd[...] = jnp.zeros_like(bwd)

    for u in range(step):
        src = at * step + u
        values, panels, picks = [], [], []
        for hi in range(his):
            slot = src * his + hi
            row, col, live = meta[0, slot], meta[1, slot], meta[2, slot]
            t = tiles[u, hi] * live.astype(jnp.float32)
            values.append(t)
            picks.append(row)
            panels.append(cols[(col // blocks), hi, col % blocks])
            flipped = jnp.concatenate(split2(t.T), axis=1)
            own = rows[u, row]
            got = jnp.dot(
                flipped, jnp.concatenate([own, own], axis=0), preferred_element_type=jnp.float32
            )
            bwd[hi, col] += got
        left = jnp.concatenate(
            [
                jnp.concatenate(
                    [t * (pick == b).astype(jnp.float32) for t, pick in zip(values, picks)], axis=1
                )
                for b in range(blocks)
            ],
            axis=0,
        )
        right = jnp.concatenate(panels, axis=0)
        high, low = split2(left)
        out = jnp.dot(high, right, preferred_element_type=jnp.float32) + jnp.dot(
            low, right, preferred_element_type=jnp.float32
        )
        fwd[u] = out.reshape(fwd.shape[1:])


def tile_products(meta, tiles, cols, rows):
    plane, his, tile, _ = tiles.shape
    blocks, width = rows.shape[1], rows.shape[3]
    span = cols.shape[0] * blocks
    step = 4
    return pl.pallas_call(
        functools.partial(tiles_kernel, his, blocks, span, step),
        grid_spec=pltpu.PrefetchScalarGridSpec(
            num_scalar_prefetch=1,
            grid=(plane // step,),
            in_specs=[
                pl.BlockSpec((step, his, tile, tile), lambda i, m: (i, 0, 0, 0)),
                pl.BlockSpec(cols.shape, lambda i, m: (0, 0, 0, 0, 0)),
                pl.BlockSpec((step, blocks, tile, width), lambda i, m: (i, 0, 0, 0)),
            ],
            out_specs=[
                pl.BlockSpec((step, blocks, tile, width), lambda i, m: (i, 0, 0, 0)),
                pl.BlockSpec((his, span, tile, width), lambda i, m: (0, 0, 0, 0)),
            ],
        ),
        out_shape=[
            jax.ShapeDtypeStruct((plane, blocks, tile, width), jnp.float32),
            jax.ShapeDtypeStruct((his, span, tile, width), jnp.float32),
        ],
        compiler_params=pltpu.CompilerParams(vmem_limit_bytes=VMEM_LIMIT),
        name="tile_products",
    )(meta, tiles, cols, rows)


def gram_kernel(sizes, first, second, product, gram, part, got, ring, whole, sent, came):
    nz, nx, ny, nc = sizes
    plane = nx * ny * nc
    group = ny * nc
    z, x, y, c = (lax.axis_index(a) for a in AXES)
    me = x * group + y * nc + c
    strip = part.shape[0] // plane

    def plane_peer(k):
        p = lax.rem(me + k, plane)
        return p, (z, p // group, lax.rem(p, group) // nc, lax.rem(p, nc))

    def ring_peer(k):
        q = lax.rem(z + k, nz)
        return q, (q, x, y, c)

    barrier = pltpu.get_barrier_semaphore()

    def greet(peer):
        def body(k, carry):
            pl.semaphore_signal(barrier, inc=1, device_id=peer(k)[1], device_id_type=MESH)
            return carry

        return body

    lax.fori_loop(1, plane, greet(plane_peer), 0)
    lax.fori_loop(1, nz, greet(ring_peer), 0)

    total = first[...] + second[...]
    product[...] = total
    part[...] = lax.dot_general(
        total, total, (((0,), (0,)), ((), ())), precision=HIGHEST, preferred_element_type=jnp.float32
    )
    pl.semaphore_wait(barrier, plane - 1 + nz - 1)

    def rows_of(p):
        return pl.ds(pl.multiple_of(p * strip, strip), strip)

    def exchange(count, peer, stage, mine, source, target):
        def copy(k, slot_of_source, slot_of_target, device):
            return pltpu.make_async_remote_copy(
                src_ref=slot_of_source,
                dst_ref=slot_of_target,
                send_sem=sent.at[stage, k],
                recv_sem=came.at[stage, mine],
                device_id=device,
                device_id_type=MESH,
            )

        def start(k, carry):
            p, device = peer(k)
            copy(k, source(p), target(mine), device).start()
            return carry

        def finish(k, carry):
            p, device = peer(k)
            copy(k, source(p), target(mine), device).wait_send()
            pltpu.make_async_remote_copy(
                src_ref=target(p),
                dst_ref=target(p),
                send_sem=sent.at[stage, k],
                recv_sem=came.at[stage, p],
                device_id=device,
                device_id_type=MESH,
            ).wait_recv()
            return carry

        lax.fori_loop(1, count, start, 0)
        lax.fori_loop(1, count, finish, 0)

    exchange(plane, plane_peer, 0, me, lambda p: part.at[rows_of(p)], lambda p: got.at[p])
    strip_sum = part[rows_of(me)]
    for k in range(1, plane):
        strip_sum = strip_sum + got[lax.rem(me + k, plane)]
    ring[z] = strip_sum
    exchange(nz, ring_peer, 1, z, lambda p: ring.at[z], lambda p: ring.at[p])
    strip_sum = ring[0]
    for k in range(1, nz):
        strip_sum = strip_sum + ring[k]
    whole[rows_of(me)] = strip_sum
    exchange(
        plane, plane_peer, 2, me, lambda p: whole.at[rows_of(me)], lambda p: whole.at[rows_of(p)]
    )
    gram[...] = whole[...]


def gram_sum(first, second):
    sizes = axis_sizes()
    plane = sizes[1] * sizes[2] * sizes[3]
    rows, width = first.shape
    strip = width // plane
    most = max(plane, sizes[0])
    vmem = pl.BlockSpec(memory_space=pltpu.VMEM)
    return pl.pallas_call(
        functools.partial(gram_kernel, sizes),
        out_shape=[
            jax.ShapeDtypeStruct((rows, width), jnp.float32),
            jax.ShapeDtypeStruct((width, width), jnp.float32),
        ],
        in_specs=[vmem, vmem],
        out_specs=[vmem, vmem],
        scratch_shapes=[
            pltpu.VMEM((width, width), jnp.float32),
            pltpu.VMEM((plane, strip, width), jnp.float32),
            pltpu.VMEM((sizes[0], strip, width), jnp.float32),
            pltpu.VMEM((width, width), jnp.float32),
            pltpu.SemaphoreType.DMA((3, most)),
            pltpu.SemaphoreType.DMA((3, most)),
        ],
        compiler_params=pltpu.CompilerParams(
            collective_id=0, has_side_effects=True, vmem_limit_bytes=VMEM_LIMIT
        ),
        name="gram_sum",
    )(first, second)


def dot_high(a, b, dims):
    return lax.dot_general(
        a, b, (dims, ((), ())), precision=HIGHEST, preferred_element_type=jnp.float32
    )


def inverse_factor(a):
    n = a.shape[0]
    sub = 8
    lanes = lax.broadcasted_iota(jnp.int32, (sub, n), 1)
    subs = lax.broadcasted_iota(jnp.int32, (sub, n), 0)
    left = [a[i * sub : (i + 1) * sub] for i in range(n // sub)]
    right = [(lanes == subs + i * sub).astype(jnp.float32) for i in range(n // sub)]
    for j in range(n):
        t0, s = divmod(j, sub)
        row = left[t0][s : s + 1]
        inv = 1.0 / row[:, j : j + 1]
        wrow = right[t0][s : s + 1]
        scaled = row * inv
        wscaled = wrow * inv
        for t in range(t0, n // sub):
            col = left[t][:, j : j + 1]
            if t == t0:
                col = jnp.where(subs[:, :1] > s, col, 0.0)
            left[t] = left[t] - col * scaled
            right[t] = right[t] - col * wscaled
    out = []
    for t in range(n // sub):
        d = jnp.sum(jnp.where(lanes == subs + t * sub, left[t], 0.0), axis=1, keepdims=True)
        out.append(right[t] * lax.rsqrt(d))
    return jnp.concatenate(out, axis=0)


def basis_kernel(scale, gram, product, basis):
    n = gram.shape[0]
    h = n // 2
    g11 = gram[:h, :h] * scale
    g21 = gram[h:, :h] * scale
    g22 = gram[h:, h:] * scale
    w11 = inverse_factor(g11)
    l21 = dot_high(g21, w11, ((1,), (1,)))
    w22 = inverse_factor(g22 - dot_high(l21, l21, ((1,), (1,))))
    w21 = -dot_high(w22, dot_high(l21, w11, ((1,), (0,))), ((1,), (0,)))
    first = product[:, :h]
    basis[:, :h] = dot_high(first, w11, ((1,), (1,)))
    basis[:, h:] = dot_high(first, w21, ((1,), (1,))) + dot_high(
        product[:, h:], w22, ((1,), (1,))
    )


def new_basis(gram, product, nodes):
    vmem = pl.BlockSpec(memory_space=pltpu.VMEM)
    return pl.pallas_call(
        functools.partial(basis_kernel, 1.0 / nodes),
        out_shape=jax.ShapeDtypeStruct(product.shape, jnp.float32),
        in_specs=[vmem, vmem],
        out_specs=vmem,
        compiler_params=pltpu.CompilerParams(vmem_limit_bytes=VMEM_LIMIT),
        name="new_basis",
    )(gram, product)


def shards(panel, lists, tiles):
    nz, nx, ny, nc = axis_sizes()
    group = ny * nc
    plane = nx * group
    tile = tiles.shape[1]
    width = panel.shape[1]
    blocks = panel.shape[0] // tile
    nodes = panel.shape[0] * nz * plane
    his = nz // group
    sort = (2, 1, 0)
    send = tiles.reshape(his, group, nx, tile, tile).transpose(2, 1, 0, 3, 4)
    here = lax.all_to_all(
        send.reshape(plane, his, tile, tile), PLANE, split_axis=0, concat_axis=0, tiled=True
    )
    send = lists.reshape(3, his, group, nx).transpose(3, 2, 1, 0)
    meta = lax.all_to_all(
        send.reshape(plane, his, 3), PLANE, split_axis=0, concat_axis=0, tiled=True
    )
    meta = meta.reshape(plane * his, 3).T
    own = panel.reshape(blocks, tile, width)
    rows = lax.all_gather(own, PLANE, axis=0)
    column = lax.all_gather(own, "z", axis=0).reshape(his, group, blocks, tile, width)
    cols = lax.all_to_all(
        column.transpose(1, 0, 2, 3, 4), GROUP, split_axis=0, concat_axis=0, tiled=True
    )
    fwd, bwd = tile_products(meta, here, cols, rows)
    first = lax.psum_scatter(fwd, PLANE, scatter_dimension=0, tiled=True)
    send = bwd.reshape(his, group, blocks, tile, width).transpose(1, 0, 2, 3, 4)
    spread = lax.all_to_all(send, GROUP, split_axis=0, concat_axis=0, tiled=True)
    spread = spread.transpose(1, 0, 2, 3, 4).reshape(nz, blocks, tile, width)
    second = lax.psum_scatter(spread, "z", scatter_dimension=0, tiled=True)
    product, gram = gram_sum(
        first.reshape(blocks * tile, width), second.reshape(blocks * tile, width)
    )
    return new_basis(gram, product, nodes)


def solution(mesh):
    sizes = mesh.devices.shape
    nx, ny, nc = grid_of(sizes)
    fine = Mesh(mesh.devices.reshape(sizes[0] // nx, nx, ny, nc), AXES)
    return jax.shard_map(
        shards,
        mesh=fine,
        in_specs=(P(AXES, None), P(None, AXES), P(AXES, None, None)),
        out_specs=P(AXES, None),
        check_vma=False,
    )


def grid_of(sizes):
    return (4, 4, 2) if sizes == (64, 8) else (2, 1, 2)
```

time: 1160 us -> 490 us (0.42)
  waiting for transfers between devices: 975 us -> 304 us
  Pallas kernels: 0 us -> 77.2 us
  other arithmetic: 58.2 us -> 0 us
  blocking collectives: 0 us -> 53 us
  matrix products: 45 us -> 0 us
  starting transfers between devices: 49.1 us -> 27.2 us
    all_to_all x3, waiting for transfers between devices: 487 us -> 31.8 us  [the longest x1 27.8 us: shards(): lax.all_to_all(column.transpose(1, 0, 2, 3, 4), GROUP, split_axis=0, conc...]
    psum x1 -> x0, waiting for transfers between devices: 453 us -> none  [shards(): gram = lax.psum(partial_gram, ('rows', 'grp')) / nodes]
    reduce_scatter x1 -> x2, waiting for transfers between devices: 0.02 us -> 194 us  [the longest x1 127 us: shards(): first = lax.psum_scatter(fwd, PLANE, scatter_dimension=0, tiled=True)]
    pallas_call x0 -> x3, Pallas kernels: none -> 77.2 us  [the longest x1 39.3 us: gram_sum(): pl.pallas_call(functools.partial(gram_kernel, sizes), out_shape=[jax.Shap...]
    another operation x9 -> x0, other arithmetic: 53.7 us -> none  [the longest x6 34 us: shards(): lower = jnp.linalg.cholesky(gram)]
    all_to_all x0 -> x1, blocking collectives: none -> 53 us  [shards(): lax.all_to_all(send, GROUP, split_axis=0, concat_axis=0, tiled=True)]
    dot_general x7 -> x0, matrix products: 43.6 us -> none  [the longest x1 11 us: shards(): jnp.einsum('sji,sjk->sik', masked, row_blocks.astype(jnp.float32), precis...]
    all_gather x1 -> x2, waiting for transfers between devices: 35 us -> 76.4 us  [the longest x1 47.9 us: shards(): lax.all_gather(own, 'z', axis=0).reshape(his, group, blocks, tile, width)]
  transfers between devices with their start and end apart: 6 -> 7, of which waited for: 4 -> 7; matrix products, arithmetic and copies ran while one was open for 4% -> 2% of each run, Pallas kernels for 0% -> 0%
where the time goes in v1:
time: 490 us
  waiting for transfers between devices  304 us (62%)
  Pallas kernels  77.2 us (16%)
  blocking collectives  53 us (11%)
  starting transfers between devices  27.2 us (6%)
  local copies, waits for them, and re-layouts  14.9 us (3%)
  between operations  13.2 us (3%)
    reduce_scatter x1, waiting for transfers between devices, shards(): first = lax.psum_scatter(fwd, PLANE, scatter_dimension=0, tiled=True)  127 us
    reduce_scatter x1, waiting for transfers between devices, shards(): second = lax.psum_scatter(spread, 'z', scatter_dimension=0, tiled=True)  67.5 us
    all_to_all x1, blocking collectives, shards(): lax.all_to_all(send, GROUP, split_axis=0, concat_axis=0, tiled=True)  53 us
    all_gather x1, waiting for transfers between devices, shards(): lax.all_gather(own, 'z', axis=0).reshape(his, group, blocks, tile, width)  47.9 us
    pallas_call x1, Pallas kernels, gram_sum(): pl.pallas_call(functools.partial(gram_kernel, sizes), out_shape=[jax.Shap...  39.3 us
    all_gather x1, waiting for transfers between devices, shards(): rows = lax.all_gather(own, PLANE, axis=0)  28.6 us
    all_to_all x1, waiting for transfers between devices, shards(): lax.all_to_all(column.transpose(1, 0, 2, 3, 4), GROUP, split_axis=0, conc...  27.8 us
    pallas_call x1, Pallas kernels, new_basis(): pl.pallas_call(functools.partial(basis_kernel, 1.0 / nodes), out_shape=ja...  24.5 us
  transfers between devices with their start and end apart: 7, of which 7 were waited for; matrix products, arithmetic and copies ran while one was open for 2% of the time, Pallas kernels for 0%

profile of v1, /device:TPU:1, one launch (start us, length us, event | category | flops | bytes accessed | tf_op | source)
XLA Modules:
  0.0 489.7 jit_solution(13293057145310006734)
XLA Ops:
  6.5 0.7 all-gather.3.cloned.1.call-update
  7.3 0.7 all-gather.5.cloned.1.call-update
  8.0 0.8 reshape.30
  8.8 0.8 copy.32
  9.6 10.4 %all-to-all-start = ((s32[32,2,3]{2,1,0:T(2,128)}), s32[32,2,3]{2,1,0:T(2,128)S(1)}, u32[]{:S(2)}, u32[]{:S(2)}) async-start(s32[32,2,3]{2,1,0:T(2,128)} %bitcast.1), calls=%async_computation | async-start | bytes 65536 | tf_op jit(solution)/shard_map/all_to_all | solution.py:290
  20.0 4.6 copy.28
  24.6 2.7 all-to-all-done
  27.4 4.8 all-to-all-start.1
  32.2 47.9 %all-gather.3.cloned.1.call-done = bf16[16,2,128,256]{3,2,1,0:T(8,128)(2,1)} async-done(((bf16[1,2,128,256]{3,2,1,0:T(8,128)(2,1)}), bf16[16,2,128,256]{3,2,1,0:T(8,128)(2,1)}) %all-gather.3.cloned.1.call-update) | async-done | bytes 2097168 | tf_op jit(solution)/shard_map/all_gather | solution.py:296
  80.1 3.1 copy.38
  83.2 1.3 all-to-all-done.1.tiles
  84.5 11.7 %all-to-all-start.2 = ((bf16[8,2,2,128,256]{4,3,2,1,0:T(8,128)(2,1)}), bf16[8,2,2,128,256]{4,3,2,1,0:T(8,128)(2,1)S(1)}, u32[]{:S(2)}, u32[]{:S(2)}) async-start(bf16[8,2,2,128,256]{4,3,2,1,0:T(8,128)(2,1)} %bitcast.21), calls=%async_computation.2 | async-start | bytes 4194304 | tf_op jit(solution)/shard_map/all_to_all | solution.py:297
  96.2 0.7 copy.33
  96.9 27.8 %all-to-all-done.2.cols = bf16[8,2,2,128,256]{4,3,2,1,0:T(8,128)(2,1)S(1)} async-done(((bf16[8,2,2,128,256]{4,3,2,1,0:T(8,128)(2,1)}), bf16[8,2,2,128,256]{4,3,2,1,0:T(8,128)(2,1)S(1)}, u32[]{:S(2)}, u32[]{:S(2)}) %all-to-all-start.2) | async-done | bytes 2097184 | tf_op jit(solution)/shard_map/all_to_all | solution.py:297
  124.7 28.6 %all-gather.5.cloned.1.call-done.rows = bf16[32,2,128,256]{3,2,1,0:T(8,128)(2,1)} async-done(((bf16[1,2,128,256]{3,2,1,0:T(8,128)(2,1)}), bf16[32,2,128,256]{3,2,1,0:T(8,128)(2,1)}) %all-gather.5.cloned.1.call-update) | async-done | bytes 4194320 | tf_op jit(solution)/shard_map/all_gather | solution.py:295
  153.2 13.4 %tile_products.1 = (f32[32,2,128,256]{3,2,1,0:T(8,128)}, f32[2,16,128,256]{3,2,1,0:T(8,128)}) custom-call(s32[3,64]{1,0:T(4,128)} %bitcast.34, f32[32,2,128,128]{3,2,1,0:T(8,128)} %all-to-all-done.1.tiles, bf16[8,2,2,128,256]{4,3,2,1,0:T(8,128)(2,1)} %copy-done, bf16[32,2,128,256]{3,2,1,0:T(8,128)(2,1)} %all-gather.5.cloned.1.call-done.rows), custom_call_target="tpu_custom_call" | custom-call | tf_op jit(solution)/shard_map/tile_products/pallas_call | solution.py:73
  166.6 2.5 copy.37
  169.1 53.0 %all_to_all.20 = f32[8,2,2,128,256]{4,3,2,1,0:T(8,128)S(1)} all-to-all(f32[8,2,2,128,256]{4,3,2,1,0:T(8,128)S(1)} %bitcast.24), channel_id=1, replica_groups=mesh['z'=16,'x'=4,'y'=4,'core'=2] {'y','core'}, dimensions={0} | all-to-all | bytes 8388608 | tf_op jit(solution)/shard_map/all_to_all | solution.py:303
  222.1 2.3 copy.31
  224.7 0.3 reduce-scatter.3.cloned.1.call-update
  225.1 67.5 %reduce-scatter.5.cloned.1.call-done = f32[1,2,128,256]{3,2,1,0:T(8,128)} async-done(((f32[16,2,128,256]{3,2,1,0:T(8,128)}), f32[1,2,128,256]{3,2,1,0:T(8,128)}) %reduce-scatter.5.cloned.1.call-update) | async-done | bytes 262160 | tf_op jit(solution)/shard_map/reduce_scatter | solution.py:305
  292.6 126.7 %reduce-scatter.3.cloned.1.call-done = f32[1,2,128,256]{3,2,1,0:T(8,128)} async-done(((f32[32,2,128,256]{3,2,1,0:T(8,128)}), f32[1,2,128,256]{3,2,1,0:T(8,128)}) %reduce-scatter.3.cloned.1.call-update) | async-done | bytes 262160 | tf_op jit(solution)/shard_map/reduce_scatter | solution.py:301
  419.3 39.3 %gram_sum.1 = (f32[256,256]{1,0:T(8,128)}, f32[256,256]{1,0:T(8,128)}) custom-call(f32[256,256]{1,0:T(8,128)} %bitcast.31, f32[256,256]{1,0:T(8,128)} %bitcast.30), custom_call_target="tpu_custom_call" | custom-call | tf_op jit(solution)/shard_map/gram_sum/pallas_call | solution.py:190
  458.6 24.5 %new_basis.1 = f32[256,256]{1,0:T(8,128)} custom-call(f32[256,256]{1,0:T(8,128)} %get-tuple-element.11.gram, f32[256,256]{1,0:T(8,128)} %get-tuple-element.12.product), custom_call_target="tpu_custom_call" | custom-call | tf_op jit(solution)/shard_map/new_basis/pallas_call | solution.py:265
  (7 shorter events, 0.3 us)
Async XLA Ops:
  6.5 73.5 %all-gather.3.cloned.1.call-start = ((), (), s32[]{:S(2)}) async-start(), calls=%async_computation.6 | async-start | bytes 2228224 | tf_op jit(solution)/shard_map/all_gather | solution.py:296
  7.3 146.0 %all-gather.5.cloned.1.call-start = ((), (), s32[]{:S(2)}) async-start(), calls=%async_computation.7 | async-start | bytes 4325376 | tf_op jit(solution)/shard_map/all_gather | solution.py:295
  9.6 17.8 %all-to-all-start = ((s32[32,2,3]{2,1,0:T(2,128)}), s32[32,2,3]{2,1,0:T(2,128)S(1)}, u32[]{:S(2)}, u32[]{:S(2)}) async-start(s32[32,2,3]{2,1,0:T(2,128)} %bitcast.1), calls=%async_computation | async-start | bytes 65536 | tf_op jit(solution)/shard_map/all_to_all | solution.py:290
  27.4 57.1 %all-to-all-start.1 = ((f32[32,2,128,128]{3,2,1,0:T(8,128)}), f32[32,2,128,128]{3,2,1,0:T(8,128)}, u32[]{:S(2)}, u32[]{:S(2)}) async-start(f32[32,2,128,128]{3,2,1,0:T(8,128)} %bitcast.23), calls=%async_computation.1 | async-start | bytes 8388608 | tf_op jit(solution)/shard_map/all_to_all | solution.py:286
  84.5 40.2 %all-to-all-start.2 = ((bf16[8,2,2,128,256]{4,3,2,1,0:T(8,128)(2,1)}), bf16[8,2,2,128,256]{4,3,2,1,0:T(8,128)(2,1)S(1)}, u32[]{:S(2)}, u32[]{:S(2)}) async-start(bf16[8,2,2,128,256]{4,3,2,1,0:T(8,128)(2,1)} %bitcast.21), calls=%async_computation.2 | async-start | bytes 4194304 | tf_op jit(solution)/shard_map/all_to_all | solution.py:297
  96.2 196.3 %reduce-scatter.5.cloned.1.call-start = ((), (), s32[]{:S(2)}) async-start(), calls=%async_computation.9 | async-start | bytes 4456448 | tf_op jit(solution)/shard_map/reduce_scatter | solution.py:305
  124.7 28.6 %copy-start = (bf16[8,2,2,128,256]{4,3,2,1,0:T(8,128)(2,1)}, bf16[8,2,2,128,256]{4,3,2,1,0:T(8,128)(2,1)S(1)}, u32[]{:S(2)}) copy-start(bf16[8,2,2,128,256]{4,3,2,1,0:T(8,128)(2,1)S(1)} %all-to-all-done.2.cols) | copy-start | bytes 6291460
  224.5 194.8 %reduce-scatter.3.cloned.1.call-start = ((), (), s32[]{:S(2)}) async-start(), calls=%async_computation.8 | async-start | bytes 8650752 | tf_op jit(solution)/shard_map/reduce_scatter | solution.py:301
Sparse Core Ops, SparseCore 0:
  9.4 70.5 all-gather.2
  83.2 69.9 all-gather.4
  224.6 67.9 reduce-scatter.4
  297.0 122.2 reduce-scatter.2

commit v2 on v1

--- a/solution.py
+++ b/solution.py
@@ -94,13 +94,51 @@
     )(meta, tiles, cols, rows)
 
 
-def gram_kernel(sizes, first, second, product, gram, part, got, ring, whole, sent, came):
+CHUNK = 64
+SKEW = 2
+
+
+def sums_kernel(
+    sizes,
+    fwd,
+    bwd,
+    product,
+    gram,
+    held,
+    keep,
+    from_core,
+    from_x,
+    from_y,
+    from_below,
+    from_above,
+    last,
+    part,
+    got,
+    ring,
+    whole,
+    local_sem,
+    chain_sent,
+    chain_came,
+    last_sent,
+    last_came,
+    plane_sent,
+    plane_came,
+    sent,
+    came,
+):
     nz, nx, ny, nc = sizes
-    plane = nx * ny * nc
     group = ny * nc
+    plane = nx * group
+    half = nz // 2
     z, x, y, c = (lax.axis_index(a) for a in AXES)
-    me = x * group + y * nc + c
+    g = y * nc + c
+    me = x * group + g
     strip = part.shape[0] // plane
+    chunks = held.shape[1]
+    per_device = last.shape[0]
+
+    def member(p):
+        return (z, x, p // nc, lax.rem(p, nc))
 
     def plane_peer(k):
         p = lax.rem(me + k, plane)
@@ -109,6 +147,16 @@
     def ring_peer(k):
         q = lax.rem(z + k, nz)
         return q, (q, x, y, c)
+
+    def remote(source, target, send_sem, recv_sem, device):
+        return pltpu.make_async_remote_copy(
+            src_ref=source,
+            dst_ref=target,
+            send_sem=send_sem,
+            recv_sem=recv_sem,
+            device_id=device,
+            device_id_type=MESH,
+        )
 
     barrier = pltpu.get_barrier_semaphore()
 
@@ -121,43 +169,188 @@
 
     lax.fori_loop(1, plane, greet(plane_peer), 0)
     lax.fori_loop(1, nz, greet(ring_peer), 0)
-
-    total = first[...] + second[...]
+    load_held = pltpu.make_async_copy(bwd, held, local_sem.at[0])
+    load_keep = pltpu.make_async_copy(fwd.at[:, c], keep, local_sem.at[1])
+    load_held.start()
+    load_keep.start()
+    pl.semaphore_wait(barrier, plane - 1 + nz - 1)
+
+    other = (z, x, y, nc - 1 - c)
+    core_copy = remote(
+        fwd.at[:, nc - 1 - c], from_core, plane_sent.at[0, 0], plane_came.at[0, 0], other
+    )
+    core_copy.start()
+
+    d0 = lax.rem(g - z + nz, nz)
+    lower = jnp.logical_and(d0 >= 1, d0 <= half)
+    hu = jnp.where(lower, 0, 1)
+    hd = 1 - hu
+    du = jnp.where(lower, d0, lax.rem(d0 + half, nz))
+    pu = half - du
+    pd = du - 1
+    target = du == half
+    above = (lax.rem(z + 1, nz), x, y, c)
+    below = (lax.rem(z + nz - 1, nz), x, y, c)
+
+    def up(j):
+        return remote(
+            held.at[hu, j], from_below.at[j], chain_sent.at[0, j], chain_came.at[0, j], above
+        )
+
+    def down(j):
+        return remote(
+            held.at[hd, j], from_above.at[j], chain_sent.at[1, j], chain_came.at[1, j], below
+        )
+
+    def scatter(j, at):
+        return remote(
+            held.at[hd, j], last.at[at], last_sent.at[j], last_came.at[at], member(j // per_device)
+        )
+
+    load_held.wait()
+
+    def step(i, carry):
+        j = i - SKEW * pu
+
+        @pl.when(jnp.logical_and(j >= 0, j < chunks))
+        def _():
+            @pl.when(pu > 0)
+            def _():
+                up(j).wait_recv()
+                held[hu, j] += from_below[j]
+
+            up(j).start()
+
+        jd = i - SKEW * pd
+
+        @pl.when(jnp.logical_and(jnp.logical_not(target), jnp.logical_and(jd >= 0, jd < chunks)))
+        def _():
+            @pl.when(pd > 0)
+            def _():
+                down(jd).wait_recv()
+                held[hd, jd] += from_above[jd]
+
+            down(jd).start()
+
+        jt = i - SKEW * half
+
+        @pl.when(jnp.logical_and(target, jnp.logical_and(jt >= 0, jt < chunks)))
+        def _():
+            up(jt).wait_recv()
+            down(jt).wait_recv()
+            held[hd, jt] += from_below[jt] + from_above[jt]
+            at = lax.rem(jt, per_device)
+
+            @pl.when(jt // per_device == g)
+            def _():
+                last[at] = held[hd, jt]
+
+            @pl.when(jt // per_device != g)
+            def _():
+                scatter(jt, at).start()
+
+        return carry
+
+    steps = chunks + SKEW * half
+    cut = (steps // 5, (3 * steps) // 4)
+    lax.fori_loop(0, cut[0], step, 0)
+
+    load_keep.wait()
+    core_copy.wait()
+
+    def x_copy(k):
+        p = lax.rem(x + k, nx)
+        return remote(
+            keep.at[pl.ds(p * ny, ny)],
+            from_x.at[x],
+            plane_sent.at[1, k],
+            plane_came.at[1, x],
+            (z, p, y, c),
+        )
+
+    def x_source(k):
+        p = lax.rem(x + k, nx)
+        return p, remote(
+            from_x.at[p], from_x.at[p], plane_sent.at[1, k], plane_came.at[1, p], (z, p, y, c)
+        )
+
+    for k in range(1, nx + 1):
+        p = lax.rem(x + k, nx)
+
+        def add_core(i, carry, p=p):
+            keep[p * ny + i] += from_core[p * ny + i]
+            return carry
+
+        lax.fori_loop(0, ny, add_core, 0)
+        if k < nx:
+            x_copy(k).start()
+
+    lax.fori_loop(cut[0], cut[1], step, 0)
+
+    for k in range(1, nx):
+        p, copy = x_source(k)
+        copy.wait_recv()
+
+        def add_x(i, carry, p=p):
+            keep[x * ny + i] += from_x[p, i]
+            return carry
+
+        lax.fori_loop(0, ny, add_x, 0)
+
+    def y_copy(k):
+        p = lax.rem(y + k, ny)
+        return remote(
+            keep.at[x * ny + p],
+            from_y.at[y],
+            plane_sent.at[2, k],
+            plane_came.at[2, y],
+            (z, x, p, c),
+        )
+
+    for k in range(1, ny):
+        y_copy(k).start()
+
+    lax.fori_loop(cut[1], steps, step, 0)
+
+    total = keep[x * ny + y]
+    for k in range(1, ny):
+        p = lax.rem(y + k, ny)
+        remote(
+            from_y.at[p], from_y.at[p], plane_sent.at[2, k], plane_came.at[2, p], (z, x, p, c)
+        ).wait_recv()
+        total = total + from_y[p]
+    holder = lax.rem(z, group)
+
+    @pl.when(holder != g)
+    def _():
+        for at in range(per_device):
+            scatter(at, at).wait_recv()
+
+    total = total + last[...].reshape(total.shape)
     product[...] = total
     part[...] = lax.dot_general(
         total, total, (((0,), (0,)), ((), ())), precision=HIGHEST, preferred_element_type=jnp.float32
     )
-    pl.semaphore_wait(barrier, plane - 1 + nz - 1)
 
     def rows_of(p):
         return pl.ds(pl.multiple_of(p * strip, strip), strip)
 
-    def exchange(count, peer, stage, mine, source, target):
-        def copy(k, slot_of_source, slot_of_target, device):
-            return pltpu.make_async_remote_copy(
-                src_ref=slot_of_source,
-                dst_ref=slot_of_target,
-                send_sem=sent.at[stage, k],
-                recv_sem=came.at[stage, mine],
-                device_id=device,
-                device_id_type=MESH,
+    def exchange(count, peer, stage, mine, source, target_of):
+        def copy(k, p, device):
+            return remote(
+                source(p), target_of(mine), sent.at[stage, k], came.at[stage, mine], device
             )
 
         def start(k, carry):
             p, device = peer(k)
-            copy(k, source(p), target(mine), device).start()
+            copy(k, p, device).start()
             return carry
 
         def finish(k, carry):
             p, device = peer(k)
-            copy(k, source(p), target(mine), device).wait_send()
-            pltpu.make_async_remote_copy(
-                src_ref=target(p),
-                dst_ref=target(p),
-                send_sem=sent.at[stage, k],
-                recv_sem=came.at[stage, p],
-                device_id=device,
-                device_id_type=MESH,
+            copy(k, p, device).wait_send()
+            remote(
+                target_of(p), target_of(p), sent.at[stage, k], came.at[stage, p], device
             ).wait_recv()
             return carry
 
@@ -179,35 +372,81 @@
     )
     gram[...] = whole[...]
 
-
-def gram_sum(first, second):
+    for k in range(1, nx):
+        x_copy(k).wait_send()
+    for k in range(1, ny):
+        y_copy(k).wait_send()
+
+    def drain(j, carry):
+        up(j).wait_send()
+
+        @pl.when(jnp.logical_not(target))
+        def _():
+            down(j).wait_send()
+
+        @pl.when(jnp.logical_and(target, j // per_device != g))
+        def _():
+            scatter(j, lax.rem(j, per_device)).wait_send()
+
+        return carry
+
+    lax.fori_loop(0, chunks, drain, 0)
+
+
+def device_sums(fwd, bwd):
     sizes = axis_sizes()
-    plane = sizes[1] * sizes[2] * sizes[3]
-    rows, width = first.shape
+    nz, nx, ny, nc = sizes
+    group = ny * nc
+    plane = nx * group
+    _, rows, width = fwd.shape
     strip = width // plane
-    most = max(plane, sizes[0])
+    most = max(plane, nz)
+    chunks = group * rows // CHUNK
+    fwd = fwd.reshape(nx * ny, nc, rows, width)
+    bwd = bwd.reshape(2, chunks, CHUNK, width)
     vmem = pl.BlockSpec(memory_space=pltpu.VMEM)
+    anywhere = pl.BlockSpec(memory_space=pl.ANY)
+
+    def buffer(*shape):
+        return pltpu.VMEM(shape, jnp.float32)
+
+    dma = pltpu.SemaphoreType.DMA
     return pl.pallas_call(
-        functools.partial(gram_kernel, sizes),
+        functools.partial(sums_kernel, sizes),
         out_shape=[
             jax.ShapeDtypeStruct((rows, width), jnp.float32),
             jax.ShapeDtypeStruct((width, width), jnp.float32),
         ],
-        in_specs=[vmem, vmem],
+        in_specs=[anywhere, anywhere],
         out_specs=[vmem, vmem],
         scratch_shapes=[
-            pltpu.VMEM((width, width), jnp.float32),
-            pltpu.VMEM((plane, strip, width), jnp.float32),
-            pltpu.VMEM((sizes[0], strip, width), jnp.float32),
-            pltpu.VMEM((width, width), jnp.float32),
-            pltpu.SemaphoreType.DMA((3, most)),
-            pltpu.SemaphoreType.DMA((3, most)),
+            buffer(2, chunks, CHUNK, width),
+            buffer(nx * ny, rows, width),
+            buffer(nx * ny, rows, width),
+            buffer(nx, ny, rows, width),
+            buffer(ny, rows, width),
+            buffer(chunks, CHUNK, width),
+            buffer(chunks, CHUNK, width),
+            buffer(rows // CHUNK, CHUNK, width),
+            buffer(width, width),
+            buffer(plane, strip, width),
+            buffer(nz, strip, width),
+            buffer(width, width),
+            dma((2,)),
+            dma((2, chunks)),
+            dma((2, chunks)),
+            dma((chunks,)),
+            dma((rows // CHUNK,)),
+            dma((3, max(nx, ny))),
+            dma((3, max(nx, ny))),
+            dma((3, most)),
+            dma((3, most)),
         ],
         compiler_params=pltpu.CompilerParams(
             collective_id=0, has_side_effects=True, vmem_limit_bytes=VMEM_LIMIT
         ),
-        name="gram_sum",
-    )(first, second)
+        name="device_sums",
+    )(fwd, bwd)
 
 
 def dot_high(a, b, dims):
@@ -298,13 +537,8 @@
         column.transpose(1, 0, 2, 3, 4), GROUP, split_axis=0, concat_axis=0, tiled=True
     )
     fwd, bwd = tile_products(meta, here, cols, rows)
-    first = lax.psum_scatter(fwd, PLANE, scatter_dimension=0, tiled=True)
-    send = bwd.reshape(his, group, blocks, tile, width).transpose(1, 0, 2, 3, 4)
-    spread = lax.all_to_all(send, GROUP, split_axis=0, concat_axis=0, tiled=True)
-    spread = spread.transpose(1, 0, 2, 3, 4).reshape(nz, blocks, tile, width)
-    second = lax.psum_scatter(spread, "z", scatter_dimension=0, tiled=True)
-    product, gram = gram_sum(
-        first.reshape(blocks * tile, width), second.reshape(blocks * tile, width)
+    product, gram = device_sums(
+        fwd.reshape(plane, blocks * tile, width), bwd.reshape(his, group * blocks * tile, width)
     )
     return new_basis(gram, product, nodes)
 

time: 490 us -> 324 us (0.66)
  waiting for transfers between devices: 304 us -> 110 us
  Pallas kernels: 77.2 us -> 163 us
  blocking collectives: 53 us -> 0 us
  local copies, waits for them, and re-layouts: 14.9 us -> 10 us
    reduce_scatter x2 -> x0, waiting for transfers between devices: 194 us -> none  [the longest x1 127 us: shards(): first = lax.psum_scatter(fwd, PLANE, scatter_dimension=0, tiled=True)]
    pallas_call x1, Pallas kernels: 39.3 us -> 125 us  [device_sums(): pl.pallas_call(functools.partial(sums_kernel, sizes), out_shape=[jax.Shap...]
    all_to_all x1 -> x0, blocking collectives: 53 us -> none  [shards(): lax.all_to_all(send, GROUP, split_axis=0, concat_axis=0, tiled=True)]
  transfers between devices with their start and end apart: 7 -> 5, of which waited for: 7 -> 5; matrix products, arithmetic and copies ran while one was open for 2% -> 3% of each run, Pallas kernels for 0% -> 0%
where the time goes in v2:
time: 324 us; the launch traced here: 323 us
  Pallas kernels  163 us (50%)
  waiting for transfers between devices  110 us (34%)
  starting transfers between devices  27 us (8%)
  between operations  13.4 us (4%)
  local copies, waits for them, and re-layouts  10 us (3%)
    pallas_call x1, Pallas kernels, device_sums(): pl.pallas_call(functools.partial(sums_kernel, sizes), out_shape=[jax.Shap...  125 us
    all_gather x1, waiting for transfers between devices, shards(): lax.all_gather(own, 'z', axis=0).reshape(his, group, blocks, tile, width)  47.9 us
    all_gather x1, waiting for transfers between devices, shards(): rows = lax.all_gather(own, PLANE, axis=0)  28.6 us
    all_to_all x1, waiting for transfers between devices, shards(): lax.all_to_all(column.transpose(1, 0, 2, 3, 4), GROUP, split_axis=0, conc...  27.8 us
    pallas_call x1, Pallas kernels, new_basis(): pl.pallas_call(functools.partial(basis_kernel, 1.0 / nodes), out_shape=ja...  24.5 us
    pallas_call x1, Pallas kernels, tile_products(): pl.pallas_call(functools.partial(tiles_kernel, his, blocks, span, step),...  13.4 us
    all_to_all x1, starting transfers between devices, shards(): lax.all_to_all(column.transpose(1, 0, 2, 3, 4), GROUP, split_axis=0, conc...  11.7 us
    all_to_all x1, starting transfers between devices, shards(): lax.all_to_all(send.reshape(plane, his, 3), PLANE, split_axis=0, concat_a...  10.4 us
  transfers between devices with their start and end apart: 5, of which 5 were waited for; matrix products, arithmetic and copies ran while one was open for 3% of the time, Pallas kernels for 0%

profile of v2, /device:TPU:1, one launch (start us, length us, event | category | flops | bytes accessed | tf_op | source)
XLA Modules:
  0.0 323.3 jit_solution(14542617239457463693)
XLA Ops:
  6.5 0.0 all-gather.3.cloned.1.call-start
  6.5 0.7 all-gather.3.cloned.1.call-update
  7.3 0.0 all-gather.5.cloned.1.call-start
  7.3 0.7 all-gather.5.cloned.1.call-update
  8.0 0.8 reshape.18
  8.8 0.8 copy.27
  9.6 10.4 %all-to-all-start = ((s32[32,2,3]{2,1,0:T(2,128)}), s32[32,2,3]{2,1,0:T(2,128)S(1)}, u32[]{:S(2)}, u32[]{:S(2)}) async-start(s32[32,2,3]{2,1,0:T(2,128)} %bitcast.1), calls=%async_computation | async-start | bytes 65536 | tf_op jit(solution)/shard_map/all_to_all | solution.py:529
  20.0 4.6 %copy.25 = f32[2,8,4,128,128]{4,3,0,1,2:T(8,128)} copy(f32[2,8,4,128,128]{4,3,2,1,0:T(8,128)} %bitcast.18) | data formatting | bytes 8388608 | tf_op jit(solution)/shard_map/reshape | solution.py:524
  24.6 2.8 all-to-all-done
  27.4 4.8 %all-to-all-start.1 = ((f32[32,2,128,128]{3,2,1,0:T(8,128)}), f32[32,2,128,128]{3,2,1,0:T(8,128)}, u32[]{:S(2)}, u32[]{:S(2)}) async-start(f32[32,2,128,128]{3,2,1,0:T(8,128)} %bitcast.15), calls=%async_computation.1 | async-start | bytes 8388608 | tf_op jit(solution)/shard_map/all_to_all | solution.py:525
  32.2 47.9 %all-gather.3.cloned.1.call-done = bf16[16,2,128,256]{3,2,1,0:T(8,128)(2,1)} async-done(((bf16[1,2,128,256]{3,2,1,0:T(8,128)(2,1)}), bf16[16,2,128,256]{3,2,1,0:T(8,128)(2,1)}) %all-gather.3.cloned.1.call-update) | async-done | bytes 2097168 | tf_op jit(solution)/shard_map/all_gather | solution.py:535
  80.1 3.2 copy.31
  83.2 1.3 all-to-all-done.1.tiles
  84.5 11.7 %all-to-all-start.2 = ((bf16[8,2,2,128,256]{4,3,2,1,0:T(8,128)(2,1)}), bf16[8,2,2,128,256]{4,3,2,1,0:T(8,128)(2,1)S(1)}, u32[]{:S(2)}, u32[]{:S(2)}) async-start(bf16[8,2,2,128,256]{4,3,2,1,0:T(8,128)(2,1)} %bitcast.14), calls=%async_computation.2 | async-start | bytes 4194304 | tf_op jit(solution)/shard_map/all_to_all | solution.py:536
  96.2 0.7 copy.28
  96.9 27.8 %all-to-all-done.2.cols = bf16[8,2,2,128,256]{4,3,2,1,0:T(8,128)(2,1)S(1)} async-done(((bf16[8,2,2,128,256]{4,3,2,1,0:T(8,128)(2,1)}), bf16[8,2,2,128,256]{4,3,2,1,0:T(8,128)(2,1)S(1)}, u32[]{:S(2)}, u32[]{:S(2)}) %all-to-all-start.2) | async-done | bytes 2097184 | tf_op jit(solution)/shard_map/all_to_all | solution.py:536
  124.7 0.0 copy-start
  124.7 28.6 %all-gather.5.cloned.1.call-done.rows = bf16[32,2,128,256]{3,2,1,0:T(8,128)(2,1)} async-done(((bf16[1,2,128,256]{3,2,1,0:T(8,128)(2,1)}), bf16[32,2,128,256]{3,2,1,0:T(8,128)(2,1)}) %all-gather.5.cloned.1.call-update) | async-done | bytes 4194320 | tf_op jit(solution)/shard_map/all_gather | solution.py:534
  153.2 0.0 copy-done
  153.2 13.4 %tile_products.1 = (f32[32,2,128,256]{3,2,1,0:T(8,128)}, f32[2,16,128,256]{3,2,1,0:T(8,128)}) custom-call(s32[3,64]{1,0:T(4,128)} %bitcast.24, f32[32,2,128,128]{3,2,1,0:T(8,128)} %all-to-all-done.1.tiles, bf16[8,2,2,128,256]{4,3,2,1,0:T(8,128)(2,1)} %copy-done, bf16[32,2,128,256]{3,2,1,0:T(8,128)(2,1)} %all-gather.5.cloned.1.call-done.rows), custom_call_target="tpu_custom_call" | custom-call | tf_op jit(solution)/shard_map/tile_products/pallas_call | solution.py:73
  166.6 125.3 %device_sums.1 = (f32[256,256]{1,0:T(8,128)}, f32[256,256]{1,0:T(8,128)}) custom-call(f32[16,2,256,256]{3,2,1,0:T(8,128)} %bitcast.16, f32[2,32,64,256]{3,2,1,0:T(8,128)} %bitcast.17), custom_call_target="tpu_custom_call" | custom-call | tf_op jit(solution)/shard_map/device_sums/pallas_call | solution.py:414
  291.9 24.5 %new_basis.1 = f32[256,256]{1,0:T(8,128)} custom-call(f32[256,256]{1,0:T(8,128)} %get-tuple-element.11.gram, f32[256,256]{1,0:T(8,128)} %get-tuple-element.12.product), custom_call_target="tpu_custom_call" | custom-call | tf_op jit(solution)/shard_map/new_basis/pallas_call | solution.py:504
Async XLA Ops:
  6.5 73.5 %all-gather.3.cloned.1.call-start = ((), (), s32[]{:S(2)}) async-start(), calls=%async_computation.3 | async-start | bytes 2228224 | tf_op jit(solution)/shard_map/all_gather | solution.py:535
  7.3 146.0 %all-gather.5.cloned.1.call-start = ((), (), s32[]{:S(2)}) async-start(), calls=%async_computation.4 | async-start | bytes 4325376 | tf_op jit(solution)/shard_map/all_gather | solution.py:534
  9.6 17.8 %all-to-all-start = ((s32[32,2,3]{2,1,0:T(2,128)}), s32[32,2,3]{2,1,0:T(2,128)S(1)}, u32[]{:S(2)}, u32[]{:S(2)}) async-start(s32[32,2,3]{2,1,0:T(2,128)} %bitcast.1), calls=%async_computation | async-start | bytes 65536 | tf_op jit(solution)/shard_map/all_to_all | solution.py:529
  27.4 57.1 %all-to-all-start.1 = ((f32[32,2,128,128]{3,2,1,0:T(8,128)}), f32[32,2,128,128]{3,2,1,0:T(8,128)}, u32[]{:S(2)}, u32[]{:S(2)}) async-start(f32[32,2,128,128]{3,2,1,0:T(8,128)} %bitcast.15), calls=%async_computation.1 | async-start | bytes 8388608 | tf_op jit(solution)/shard_map/all_to_all | solution.py:525
  84.5 40.2 %all-to-all-start.2 = ((bf16[8,2,2,128,256]{4,3,2,1,0:T(8,128)(2,1)}), bf16[8,2,2,128,256]{4,3,2,1,0:T(8,128)(2,1)S(1)}, u32[]{:S(2)}, u32[]{:S(2)}) async-start(bf16[8,2,2,128,256]{4,3,2,1,0:T(8,128)(2,1)} %bitcast.14), calls=%async_computation.2 | async-start | bytes 4194304 | tf_op jit(solution)/shard_map/all_to_all | solution.py:536
  124.7 28.6 %copy-start = (bf16[8,2,2,128,256]{4,3,2,1,0:T(8,128)(2,1)}, bf16[8,2,2,128,256]{4,3,2,1,0:T(8,128)(2,1)S(1)}, u32[]{:S(2)}) copy-start(bf16[8,2,2,128,256]{4,3,2,1,0:T(8,128)(2,1)S(1)} %all-to-all-done.2.cols) | copy-start | bytes 6291460
Sparse Core Ops, SparseCore 0:
  9.4 70.5 all-gather.2
  83.2 69.9 all-gather.4

commit v3 on v2

--- a/solution.py
+++ b/solution.py
@@ -11,8 +11,6 @@
 MESH = pl.DeviceIdType.MESH
 VMEM_LIMIT = 56 * 1024 * 1024
 AXES = ("z", "x", "y", "core")
-PLANE = ("x", "y", "core")
-GROUP = ("y", "core")
 
 
 def axis_sizes():
@@ -23,6 +21,335 @@
     high = t.astype(jnp.bfloat16)
     low = (t - high.astype(jnp.float32)).astype(jnp.bfloat16)
     return high, low
+
+
+PASS = 2
+
+
+def bring_kernel(
+    sizes,
+    panel,
+    lists,
+    tiles,
+    here,
+    meta,
+    cols,
+    rows,
+    local_sem,
+    tile_sent,
+    tile_came,
+    list_sent,
+    list_came,
+    gather_sent,
+    gather_came,
+    chain_sent,
+    chain_came,
+    first_sent,
+    first_came,
+    second_sent,
+    second_came,
+    core_sent,
+    core_came,
+):
+    nz, nx, ny, nc = sizes
+    group = ny * nc
+    plane = nx * group
+    half = nz // 2
+    z, x, y, c = (lax.axis_index(a) for a in AXES)
+    g = y * nc + c
+    me = x * group + g
+    blocks = panel.shape[0]
+    chunks = cols.shape[1]
+
+    def member(p):
+        return (z, x, p // nc, lax.rem(p, nc))
+
+    def plane_peer(k):
+        p = lax.rem(me + k, plane)
+        return p, (z, p // group, lax.rem(p, group) // nc, lax.rem(p, nc))
+
+    def remote(source, target, send_sem, recv_sem, device):
+        return pltpu.make_async_remote_copy(
+            src_ref=source,
+            dst_ref=target,
+            send_sem=send_sem,
+            recv_sem=recv_sem,
+            device_id=device,
+            device_id_type=MESH,
+        )
+
+    above = (lax.rem(z + 1, nz), x, y, c)
+    below = (lax.rem(z + nz - 1, nz), x, y, c)
+    other = (z, x, y, nc - 1 - c)
+
+    barrier = pltpu.get_barrier_semaphore()
+
+    def greet(k, carry):
+        pl.semaphore_signal(barrier, inc=1, device_id=plane_peer(k)[1], device_id_type=MESH)
+        return carry
+
+    lax.fori_loop(1, plane, greet, 0)
+    for device in (above, below):
+        pl.semaphore_signal(barrier, inc=1, device_id=device, device_id_type=MESH)
+
+    holder = lax.rem(z, group)
+    his = z // group
+    place = g * nx + x
+    local = [
+        pltpu.make_async_copy(panel, rows.at[x, y, c], local_sem.at[0]),
+        pltpu.make_async_copy(tiles.at[:, place], here.at[me], local_sem.at[1]),
+        pltpu.make_async_copy(lists, meta.at[me], local_sem.at[2]),
+    ]
+    to_cols = pltpu.make_async_copy(
+        panel, cols.at[his, pl.ds(g * blocks, blocks)], local_sem.at[3]
+    )
+    for copy in local:
+        copy.start()
+
+    @pl.when(holder == g)
+    def _():
+        to_cols.start()
+
+    pl.semaphore_wait(barrier, plane - 1 + 2)
+
+    def gather(p):
+        return remote(
+            panel,
+            cols.at[his, pl.ds(p * blocks, blocks)],
+            gather_sent.at[0],
+            gather_came.at[p],
+            member(holder),
+        )
+
+    @pl.when(holder != g)
+    def _():
+        gather(g).start()
+
+    def first_x(k, p, at):
+        return remote(
+            panel.at[0], rows.at[at, y, c, 0], first_sent.at[0, k], first_came.at[0, at], (z, p, y, c)
+        )
+
+    def first_y(k, p, at):
+        return remote(
+            panel.at[1], rows.at[x, at, c, 1], first_sent.at[1, k], first_came.at[1, at], (z, x, p, c)
+        )
+
+    for k in range(1, nx):
+        first_x(k, lax.rem(x + k, nx), x).start()
+    for k in range(1, ny):
+        first_y(k, lax.rem(y + k, ny), y).start()
+
+    def tile_copy(k, p, device, at):
+        to = lax.rem(p, group) * nx + p // group
+        return remote(tiles.at[:, to], here.at[at], tile_sent.at[k], tile_came.at[at], device)
+
+    def list_copy(k, device, at):
+        return remote(lists, meta.at[at], list_sent.at[k], list_came.at[at], device)
+
+    def start_tiles(k, carry):
+        p, device = plane_peer(k)
+        list_copy(k, device, me).start()
+        tile_copy(k, p, device, me).start()
+        return carry
+
+    lax.fori_loop(1, plane, start_tiles, 0)
+
+    d0 = lax.rem(g - z + nz, nz)
+    lower = jnp.logical_and(d0 >= 1, d0 <= half)
+    hu = jnp.where(lower, 0, 1)
+    hd = 1 - hu
+    du = jnp.where(lower, d0, lax.rem(d0 + half, nz))
+    dd = half - du
+    origin = du == half
+
+    def down(h, j):
+        return remote(
+            cols.at[h, j], cols.at[h, j], chain_sent.at[0, j], chain_came.at[0, j], below
+        )
+
+    def up(h, j):
+        return remote(
+            cols.at[h, j], cols.at[h, j], chain_sent.at[1, j], chain_came.at[1, j], above
+        )
+
+    @pl.when(origin)
+    def _():
+        to_cols.wait()
+        for p in range(group):
+
+            @pl.when(p != g)
+            def _(p=p):
+                gather(p).wait_recv()
+
+        def begin(j, carry):
+            down(hd, j).start()
+            up(hd, j).start()
+            return carry
+
+        lax.fori_loop(0, chunks, begin, 0)
+
+    def step(i, carry):
+        j = i - PASS * (du - 1)
+
+        @pl.when(jnp.logical_and(j >= 0, j < chunks))
+        def _():
+            down(hu, j).wait_recv()
+
+            @pl.when(du < half)
+            def _():
+                down(hu, j).start()
+
+        ju = i - PASS * (dd - 1)
+
+        @pl.when(jnp.logical_and(jnp.logical_not(origin), jnp.logical_and(ju >= 0, ju < chunks)))
+        def _():
+            up(hd, ju).wait_recv()
+
+            @pl.when(dd < half - 1)
+            def _():
+                up(hd, ju).start()
+
+        return carry
+
+    steps = chunks + PASS * (half - 1)
+    cut = (steps // 3, (2 * steps) // 3)
+    lax.fori_loop(0, cut[0], step, 0)
+
+    def second_y(k, p, at):
+        part = rows.at[:, at, c, 0]
+        return remote(part, part, second_sent.at[0, k], second_came.at[0, at], (z, x, p, c))
+
+    def second_x(k, p, at):
+        part = rows.at[at, :, c, 1]
+        return remote(part, part, second_sent.at[1, k], second_came.at[1, at], (z, p, y, c))
+
+    for copy in local:
+        copy.wait()
+    for k in range(1, nx):
+        p = lax.rem(x + k, nx)
+        first_x(k, p, p).wait_recv()
+    for k in range(1, ny):
+        second_y(k, lax.rem(y + k, ny), y).start()
+    for k in range(1, ny):
+        p = lax.rem(y + k, ny)
+        first_y(k, p, p).wait_recv()
+    for k in range(1, nx):
+        second_x(k, lax.rem(x + k, nx), x).start()
+
+    lax.fori_loop(cut[0], cut[1], step, 0)
+
+    def core_y(p, of):
+        part = rows.at[:, p, of, 0]
+        return remote(part, part, core_sent.at[0, p], core_came.at[0, p], other)
+
+    def core_x(p, of):
+        part = rows.at[p, :, of, 1]
+        return remote(part, part, core_sent.at[1, p], core_came.at[1, p], other)
+
+    core_y(y, c).start()
+    core_x(x, c).start()
+    for k in range(1, ny):
+        p = lax.rem(y + k, ny)
+        second_y(k, p, p).wait_recv()
+        core_y(p, c).start()
+    for k in range(1, nx):
+        p = lax.rem(x + k, nx)
+        second_x(k, p, p).wait_recv()
+        core_x(p, c).start()
+
+    lax.fori_loop(cut[1], steps, step, 0)
+
+    def finish(k, carry):
+        p, device = plane_peer(k)
+        tile_copy(k, p, device, p).wait_recv()
+        list_copy(k, device, p).wait_recv()
+        tile_copy(k, p, device, me).wait_send()
+        list_copy(k, device, me).wait_send()
+        return carry
+
+    lax.fori_loop(1, plane, finish, 0)
+    for p in range(ny):
+        core_y(p, nc - 1 - c).wait_recv()
+        core_y(p, c).wait_send()
+    for p in range(nx):
+        core_x(p, nc - 1 - c).wait_recv()
+        core_x(p, c).wait_send()
+    for k in range(1, nx):
+        p = lax.rem(x + k, nx)
+        first_x(k, p, x).wait_send()
+        second_x(k, p, x).wait_send()
+    for k in range(1, ny):
+        p = lax.rem(y + k, ny)
+        first_y(k, p, y).wait_send()
+        second_y(k, p, y).wait_send()
+
+    @pl.when(holder != g)
+    def _():
+        gather(g).wait_send()
+
+    def drain(j, carry):
+        @pl.when(origin)
+        def _():
+            down(hd, j).wait_send()
+            up(hd, j).wait_send()
+
+        @pl.when(du < half)
+        def _():
+            down(hu, j).wait_send()
+
+        @pl.when(jnp.logical_and(jnp.logical_not(origin), dd < half - 1))
+        def _():
+            up(hd, j).wait_send()
+
+        return carry
+
+    lax.fori_loop(0, chunks, drain, 0)
+
+
+def bring(panel, lists, tiles):
+    sizes = axis_sizes()
+    nz, nx, ny, nc = sizes
+    group = ny * nc
+    plane = nx * group
+    blocks, tile, width = panel.shape
+    his = nz // group
+    span = group * blocks
+    anywhere = pl.BlockSpec(memory_space=pl.ANY)
+    dma = pltpu.SemaphoreType.DMA
+    most = max(nx, ny)
+    return pl.pallas_call(
+        functools.partial(bring_kernel, sizes),
+        out_shape=[
+            jax.ShapeDtypeStruct((plane, his, tile, tile), jnp.float32),
+            jax.ShapeDtypeStruct((plane,) + lists.shape, jnp.int32),
+            jax.ShapeDtypeStruct((his, span, tile, width), jnp.bfloat16),
+            jax.ShapeDtypeStruct((nx, ny, nc, blocks, tile, width), jnp.bfloat16),
+        ],
+        in_specs=[anywhere] * 3,
+        out_specs=[anywhere] * 4,
+        scratch_shapes=[
+            dma((4,)),
+            dma((plane,)),
+            dma((plane,)),
+            dma((plane,)),
+            dma((plane,)),
+            dma((1,)),
+            dma((group,)),
+            dma((2, span)),
+            dma((2, span)),
+            dma((2, most)),
+            dma((2, most)),
+            dma((2, most)),
+            dma((2, most)),
+            dma((2, most)),
+            dma((2, most)),
+        ],
+        compiler_params=pltpu.CompilerParams(
+            collective_id=1, has_side_effects=True, vmem_limit_bytes=VMEM_LIMIT
+        ),
+        name="bring",
+    )(panel, lists, tiles)
 
 
 def tiles_kernel(his, blocks, span, step, meta, tiles, cols, rows, fwd, bwd):
@@ -41,7 +368,7 @@
             t = tiles[u, hi] * live.astype(jnp.float32)
             values.append(t)
             picks.append(row)
-            panels.append(cols[(col // blocks), hi, col % blocks])
+            panels.append(cols[hi, col])
             flipped = jnp.concatenate(split2(t.T), axis=1)
             own = rows[u, row]
             got = jnp.dot(
@@ -68,7 +395,7 @@
 def tile_products(meta, tiles, cols, rows):
     plane, his, tile, _ = tiles.shape
     blocks, width = rows.shape[1], rows.shape[3]
-    span = cols.shape[0] * blocks
+    span = cols.shape[1]
     step = 4
     return pl.pallas_call(
         functools.partial(tiles_kernel, his, blocks, span, step),
@@ -77,7 +404,7 @@
             grid=(plane // step,),
             in_specs=[
                 pl.BlockSpec((step, his, tile, tile), lambda i, m: (i, 0, 0, 0)),
-                pl.BlockSpec(cols.shape, lambda i, m: (0, 0, 0, 0, 0)),
+                pl.BlockSpec(cols.shape, lambda i, m: (0, 0, 0, 0)),
                 pl.BlockSpec((step, blocks, tile, width), lambda i, m: (i, 0, 0, 0)),
             ],
             out_specs=[
@@ -520,22 +847,17 @@
     blocks = panel.shape[0] // tile
     nodes = panel.shape[0] * nz * plane
     his = nz // group
-    sort = (2, 1, 0)
-    send = tiles.reshape(his, group, nx, tile, tile).transpose(2, 1, 0, 3, 4)
-    here = lax.all_to_all(
-        send.reshape(plane, his, tile, tile), PLANE, split_axis=0, concat_axis=0, tiled=True
+    own = panel.reshape(blocks, tile, width)
+    here, meta, cols, rows = bring(
+        own,
+        jnp.pad(lists, ((0, 8 - 3), (0, 128 - lists.shape[1] % 128))),
+        tiles.reshape(his, group * nx, tile, tile),
     )
-    send = lists.reshape(3, his, group, nx).transpose(3, 2, 1, 0)
-    meta = lax.all_to_all(
-        send.reshape(plane, his, 3), PLANE, split_axis=0, concat_axis=0, tiled=True
-    )
-    meta = meta.reshape(plane * his, 3).T
-    own = panel.reshape(blocks, tile, width)
-    rows = lax.all_gather(own, PLANE, axis=0)
-    column = lax.all_gather(own, "z", axis=0).reshape(his, group, blocks, tile, width)
-    cols = lax.all_to_all(
-        column.transpose(1, 0, 2, 3, 4), GROUP, split_axis=0, concat_axis=0, tiled=True
-    )
+    place = (lax.axis_index("y") * nc + lax.axis_index("core")) * nx + lax.axis_index("x")
+    meta = meta[:, :3, : lists.shape[1]].reshape(plane, 3, his, group * nx)
+    meta = lax.dynamic_index_in_dim(meta, place, 3, keepdims=False)
+    meta = meta.transpose(1, 0, 2).reshape(3, plane * his)
+    rows = rows.reshape(plane, blocks, tile, width)
     fwd, bwd = tile_products(meta, here, cols, rows)
     product, gram = device_sums(
         fwd.reshape(plane, blocks * tile, width), bwd.reshape(his, group * blocks * tile, width)

time: 324 us -> 300 us (0.926)
  Pallas kernels: 163 us -> 296 us
  waiting for transfers between devices: 110 us -> 0 us
  starting transfers between devices: 27 us -> 0 us
  between operations: 13.4 us -> 0.05 us
  local copies, waits for them, and re-layouts: 10 us -> 3.38 us
    pallas_call x0 -> x1, Pallas kernels: none -> 118 us  [bring(): pl.pallas_call(functools.partial(bring_kernel, sizes), out_shape=[jax.Sha...]
    all_gather x2 -> x0, waiting for transfers between devices: 76.4 us -> none  [the longest x1 47.9 us: shards(): lax.all_gather(own, 'z', axis=0).reshape(his, group, blocks, tile, width)]
    all_to_all x3 -> x0, waiting for transfers between devices: 31.8 us -> none  [the longest x1 27.8 us: shards(): lax.all_to_all(column.transpose(1, 0, 2, 3, 4), GROUP, split_axis=0, conc...]
    all_to_all x3 -> x0, starting transfers between devices: 27 us -> none  [the longest x1 11.7 us: shards(): lax.all_to_all(column.transpose(1, 0, 2, 3, 4), GROUP, split_axis=0, conc...]
    pallas_call x1, Pallas kernels: 125 us -> 140 us  [device_sums(): pl.pallas_call(functools.partial(sums_kernel, sizes), out_shape=[jax.Shap...]
    reshape x5 -> x2, local copies, waits for them, and re-layouts: 10 us -> 0.82 us  [the longest x1 0.71 us: shards(): meta = meta.transpose(1, 0, 2).reshape(3, plane * his)]
  transfers between devices with their start and end apart: 5 -> 0, of which waited for: 5 -> 0; matrix products, arithmetic and copies ran while one was open for 3% -> 0% of each run, Pallas kernels for 0% -> 0%
where the time goes in v3:
time: 300 us; the launch traced here: 299 us
  Pallas kernels  296 us (99%)
  local copies, waits for them, and re-layouts  3.38 us (1%)
    pallas_call x1, Pallas kernels, device_sums(): pl.pallas_call(functools.partial(sums_kernel, sizes), out_shape=[jax.Shap...  140 us
    pallas_call x1, Pallas kernels, bring(): pl.pallas_call(functools.partial(bring_kernel, sizes), out_shape=[jax.Sha...  118 us
    pallas_call x1, Pallas kernels, new_basis(): pl.pallas_call(functools.partial(basis_kernel, 1.0 / nodes), out_shape=ja...  24.5 us
    pallas_call x1, Pallas kernels, tile_products(): pl.pallas_call(functools.partial(tiles_kernel, his, blocks, span, step),...  13.3 us

profile of v3, /device:TPU:1, one launch (start us, length us, event | category | flops | bytes accessed | tf_op | source)
XLA Modules:
  0.0 299.2 jit_solution(13719520516847965304)
XLA Ops:
  0.0 1.3 pad.4.lists
  1.3 118.0 %bring.1 = (f32[32,2,128,128]{3,2,1,0:T(8,128)}, s32[32,8,128]{2,1,0:T(8,128)}, bf16[2,16,128,256]{3,2,1,0:T(8,128)(2,1)}, bf16[4,4,2,2,128,256]{5,4,3,2,1,0:T(8,128)(2,1)}) custom-call(bf16[2,128,256]{2,1,0:T(8,128)(2,1)} %bitcast.14, s32[8,128]{1,0:T(8,128)} %pad.4.lists, f32[2,32,128,128]{3,2,1,0:T(8,128)} %bitcast.12), custom_call_target="tpu_custom_call" | custom-call | tf_op jit(solution)/shard_map/bring/pallas_call | solution.py:321
  119.3 0.9 slice.3
  120.2 0.1 reshape.17
  120.3 0.2 constant_dynamic-slice_fusion
  120.5 0.1 copy.7
  120.6 0.1 copy.8
  120.7 0.7 reshape.18.meta
  121.4 13.3 %tile_products.1 = (f32[32,2,128,256]{3,2,1,0:T(8,128)}, f32[2,16,128,256]{3,2,1,0:T(8,128)}) custom-call(s32[3,64]{1,0:T(4,128)} %reshape.18.meta, f32[32,2,128,128]{3,2,1,0:T(8,128)} %get-tuple-element.14.tiles, bf16[2,16,128,256]{3,2,1,0:T(8,128)(2,1)} %get-tuple-element.15.cols, bf16[32,2,128,256]{3,2,1,0:T(8,128)(2,1)} %bitcast.13), custom_call_target="tpu_custom_call" | custom-call | tf_op jit(solution)/shard_map/tile_products/pallas_call | solution.py:400
  134.7 139.9 %device_sums.1 = (f32[256,256]{1,0:T(8,128)}, f32[256,256]{1,0:T(8,128)}) custom-call(f32[16,2,256,256]{3,2,1,0:T(8,128)} %bitcast.10, f32[2,32,64,256]{3,2,1,0:T(8,128)} %bitcast.11), custom_call_target="tpu_custom_call" | custom-call | tf_op jit(solution)/shard_map/device_sums/pallas_call | solution.py:741
  274.6 24.5 %new_basis.1 = f32[256,256]{1,0:T(8,128)} custom-call(f32[256,256]{1,0:T(8,128)} %get-tuple-element.19.gram, f32[256,256]{1,0:T(8,128)} %get-tuple-element.20.product), custom_call_target="tpu_custom_call" | custom-call | tf_op jit(solution)/shard_map/new_basis/pallas_call | solution.py:831
  (1 shorter events, 0.0 us)

commit v4 on v3

--- a/solution.py
+++ b/solution.py
@@ -23,7 +23,7 @@
     return high, low
 
 
-PASS = 2
+PASS = 3
 
 
 def bring_kernel(
@@ -65,8 +65,11 @@
         return (z, x, p // nc, lax.rem(p, nc))
 
     def plane_peer(k):
-        p = lax.rem(me + k, plane)
-        return p, (z, p // group, lax.rem(p, group) // nc, lax.rem(p, nc))
+        across = lax.rem(k, nx)
+        px = lax.rem(x + across, nx)
+        py = lax.rem(y + lax.rem(k // nx, ny) + across, ny)
+        pc = lax.rem(c + k // (nx * ny), nc)
+        return px * group + py * nc + pc, (z, px, py, pc)
 
     def remote(source, target, send_sem, recv_sem, device):
         return pltpu.make_async_remote_copy(
@@ -173,42 +176,39 @@
             cols.at[h, j], cols.at[h, j], chain_sent.at[1, j], chain_came.at[1, j], above
         )
 
+    def in_turn(j):
+        return lax.rem(g + j // blocks, group) * blocks + lax.rem(j, blocks)
+
     @pl.when(origin)
     def _():
         to_cols.wait()
-        for p in range(group):
-
-            @pl.when(p != g)
-            def _(p=p):
-                gather(p).wait_recv()
-
-        def begin(j, carry):
-            down(hd, j).start()
-            up(hd, j).start()
-            return carry
-
-        lax.fori_loop(0, chunks, begin, 0)
+        for m in range(group):
+            if m > 0:
+                gather(lax.rem(g + m, group)).wait_recv()
+            for b in range(blocks):
+                down(hd, in_turn(m * blocks + b)).start()
+                up(hd, in_turn(m * blocks + b)).start()
 
     def step(i, carry):
         j = i - PASS * (du - 1)
 
         @pl.when(jnp.logical_and(j >= 0, j < chunks))
         def _():
-            down(hu, j).wait_recv()
+            down(hu, in_turn(j)).wait_recv()
 
             @pl.when(du < half)
             def _():
-                down(hu, j).start()
+                down(hu, in_turn(j)).start()
 
         ju = i - PASS * (dd - 1)
 
         @pl.when(jnp.logical_and(jnp.logical_not(origin), jnp.logical_and(ju >= 0, ju < chunks)))
         def _():
-            up(hd, ju).wait_recv()
+            up(hd, in_turn(ju)).wait_recv()
 
             @pl.when(dd < half - 1)
             def _():
-                up(hd, ju).start()
+                up(hd, in_turn(ju)).start()
 
         return carry
 
@@ -422,7 +422,7 @@
 
 
 CHUNK = 64
-SKEW = 2
+SKEW = 3
 
 
 def sums_kernel(

time: 300 us -> 260 us (0.87)
  Pallas kernels: 296 us -> 256 us
    pallas_call x1, Pallas kernels: 118 us -> 98 us  [bring(): pl.pallas_call(functools.partial(bring_kernel, sizes), out_shape=[jax.Sha...]
    pallas_call x1, Pallas kernels: 140 us -> 120 us  [device_sums(): pl.pallas_call(functools.partial(sums_kernel, sizes), out_shape=[jax.Shap...]
where the time goes in v4:
time: 260 us
  Pallas kernels  256 us (98%)
  local copies, waits for them, and re-layouts  3.38 us (1%)
    pallas_call x1, Pallas kernels, device_sums(): pl.pallas_call(functools.partial(sums_kernel, sizes), out_shape=[jax.Shap...  120 us
    pallas_call x1, Pallas kernels, bring(): pl.pallas_call(functools.partial(bring_kernel, sizes), out_shape=[jax.Sha...  98 us
    pallas_call x1, Pallas kernels, new_basis(): pl.pallas_call(functools.partial(basis_kernel, 1.0 / nodes), out_shape=ja...  24.5 us
    pallas_call x1, Pallas kernels, tile_products(): pl.pallas_call(functools.partial(tiles_kernel, his, blocks, span, step),...  13.4 us

profile of v4, /device:TPU:1, one launch (start us, length us, event | category | flops | bytes accessed | tf_op | source)
XLA Modules:
  0.0 259.7 jit_solution(4891837518692069511)
XLA Ops:
  0.0 1.3 pad.4.lists
  1.3 98.0 %bring.1 = (f32[32,2,128,128]{3,2,1,0:T(8,128)}, s32[32,8,128]{2,1,0:T(8,128)}, bf16[2,16,128,256]{3,2,1,0:T(8,128)(2,1)}, bf16[4,4,2,2,128,256]{5,4,3,2,1,0:T(8,128)(2,1)}) custom-call(bf16[2,128,256]{2,1,0:T(8,128)(2,1)} %bitcast.14, s32[8,128]{1,0:T(8,128)} %pad.4.lists, f32[2,32,128,128]{3,2,1,0:T(8,128)} %bitcast.12), custom_call_target="tpu_custom_call" | custom-call | tf_op jit(solution)/shard_map/bring/pallas_call | solution.py:321
  99.3 0.9 slice.3
  100.2 0.1 reshape.17
  100.4 0.2 constant_dynamic-slice_fusion
  100.5 0.1 copy.7
  100.6 0.1 copy.8
  100.7 0.7 reshape.18.meta
  101.4 13.4 %tile_products.1 = (f32[32,2,128,256]{3,2,1,0:T(8,128)}, f32[2,16,128,256]{3,2,1,0:T(8,128)}) custom-call(s32[3,64]{1,0:T(4,128)} %reshape.18.meta, f32[32,2,128,128]{3,2,1,0:T(8,128)} %get-tuple-element.14.tiles, bf16[2,16,128,256]{3,2,1,0:T(8,128)(2,1)} %get-tuple-element.15.cols, bf16[32,2,128,256]{3,2,1,0:T(8,128)(2,1)} %bitcast.13), custom_call_target="tpu_custom_call" | custom-call | tf_op jit(solution)/shard_map/tile_products/pallas_call | solution.py:400
  114.8 120.4 %device_sums.1 = (f32[256,256]{1,0:T(8,128)}, f32[256,256]{1,0:T(8,128)}) custom-call(f32[16,2,256,256]{3,2,1,0:T(8,128)} %bitcast.10, f32[2,32,64,256]{3,2,1,0:T(8,128)} %bitcast.11), custom_call_target="tpu_custom_call" | custom-call | tf_op jit(solution)/shard_map/device_sums/pallas_call | solution.py:741
  235.2 24.5 %new_basis.1 = f32[256,256]{1,0:T(8,128)} custom-call(f32[256,256]{1,0:T(8,128)} %get-tuple-element.19.gram, f32[256,256]{1,0:T(8,128)} %get-tuple-element.20.product), custom_call_target="tpu_custom_call" | custom-call | tf_op jit(solution)/shard_map/new_basis/pallas_call | solution.py:831
  (1 shorter events, 0.0 us)

commit v5 on v4

--- a/solution.py
+++ b/solution.py
@@ -23,6 +23,7 @@
     return high, low
 
 
+CODE_TOP = 32767.0
 PASS = 3
 
 
@@ -35,6 +36,9 @@
     meta,
     cols,
     rows,
+    stage,
+    coded,
+    message,
     local_sem,
     tile_sent,
     tile_came,
@@ -97,17 +101,17 @@
 
     holder = lax.rem(z, group)
     his = z // group
-    place = g * nx + x
     local = [
         pltpu.make_async_copy(panel, rows.at[x, y, c], local_sem.at[0]),
-        pltpu.make_async_copy(tiles.at[:, place], here.at[me], local_sem.at[1]),
-        pltpu.make_async_copy(lists, meta.at[me], local_sem.at[2]),
+        pltpu.make_async_copy(coded.at[me], here.at[me], local_sem.at[1]),
+        pltpu.make_async_copy(message.at[me], meta.at[me], local_sem.at[2]),
     ]
+    load = pltpu.make_async_copy(tiles, stage, local_sem.at[4])
+    load.start()
     to_cols = pltpu.make_async_copy(
         panel, cols.at[his, pl.ds(g * blocks, blocks)], local_sem.at[3]
     )
-    for copy in local:
-        copy.start()
+    local[0].start()
 
     @pl.when(holder == g)
     def _():
@@ -144,19 +148,34 @@
         first_y(k, lax.rem(y + k, ny), y).start()
 
     def tile_copy(k, p, device, at):
+        return remote(coded.at[p], here.at[at], tile_sent.at[k], tile_came.at[at], device)
+
+    def list_copy(k, p, device, at):
+        return remote(message.at[p], meta.at[at], list_sent.at[k], list_came.at[at], device)
+
+    def code(p):
         to = lax.rem(p, group) * nx + p // group
-        return remote(tiles.at[:, to], here.at[at], tile_sent.at[k], tile_came.at[at], device)
-
-    def list_copy(k, device, at):
-        return remote(lists, meta.at[at], list_sent.at[k], list_came.at[at], device)
+        entry = lists[p]
+        for h in range(tiles.shape[0]):
+            t = stage[h, to]
+            top = jnp.maximum(jnp.max(jnp.abs(t), axis=0, keepdims=True), 1e-30)
+            coded[p, h] = jnp.round(t * (CODE_TOP / top)).astype(jnp.int32).astype(jnp.int16)
+            line = lax.broadcasted_iota(jnp.int32, entry.shape, 0)
+            entry = jnp.where(line == h, top * (1.0 / CODE_TOP), entry)
+        message[p] = entry
 
     def start_tiles(k, carry):
         p, device = plane_peer(k)
-        list_copy(k, device, me).start()
+        code(p)
+        list_copy(k, p, device, me).start()
         tile_copy(k, p, device, me).start()
         return carry
 
+    load.wait()
     lax.fori_loop(1, plane, start_tiles, 0)
+    code(me)
+    local[1].start()
+    local[2].start()
 
     d0 = lax.rem(g - z + nz, nz)
     lower = jnp.logical_and(d0 >= 1, d0 <= half)
@@ -263,9 +282,9 @@
     def finish(k, carry):
         p, device = plane_peer(k)
         tile_copy(k, p, device, p).wait_recv()
-        list_copy(k, device, p).wait_recv()
+        list_copy(k, p, device, p).wait_recv()
         tile_copy(k, p, device, me).wait_send()
-        list_copy(k, device, me).wait_send()
+        list_copy(k, p, device, me).wait_send()
         return carry
 
     lax.fori_loop(1, plane, finish, 0)
@@ -321,15 +340,18 @@
     return pl.pallas_call(
         functools.partial(bring_kernel, sizes),
         out_shape=[
-            jax.ShapeDtypeStruct((plane, his, tile, tile), jnp.float32),
-            jax.ShapeDtypeStruct((plane,) + lists.shape, jnp.int32),
+            jax.ShapeDtypeStruct((plane, his, tile, tile), jnp.int16),
+            jax.ShapeDtypeStruct(lists.shape, jnp.float32),
             jax.ShapeDtypeStruct((his, span, tile, width), jnp.bfloat16),
             jax.ShapeDtypeStruct((nx, ny, nc, blocks, tile, width), jnp.bfloat16),
         ],
-        in_specs=[anywhere] * 3,
+        in_specs=[anywhere, pl.BlockSpec(memory_space=pltpu.VMEM), anywhere],
         out_specs=[anywhere] * 4,
         scratch_shapes=[
-            dma((4,)),
+            pltpu.VMEM(tiles.shape, jnp.float32),
+            pltpu.VMEM((plane, his, tile, tile), jnp.int16),
+            pltpu.VMEM(lists.shape, jnp.float32),
+            dma((5,)),
             dma((plane,)),
             dma((plane,)),
             dma((plane,)),
@@ -352,7 +374,7 @@
     )(panel, lists, tiles)
 
 
-def tiles_kernel(his, blocks, span, step, meta, tiles, cols, rows, fwd, bwd):
+def tiles_kernel(his, blocks, span, step, meta, tiles, scales, cols, rows, fwd, bwd):
     at = pl.program_id(0)
 
     @pl.when(at == 0)
@@ -365,7 +387,8 @@
         for hi in range(his):
             slot = src * his + hi
             row, col, live = meta[0, slot], meta[1, slot], meta[2, slot]
-            t = tiles[u, hi] * live.astype(jnp.float32)
+            scale = scales[u, hi : hi + 1] * live.astype(jnp.float32)
+            t = tiles[u, hi].astype(jnp.int32).astype(jnp.float32) * scale
             values.append(t)
             picks.append(row)
             panels.append(cols[hi, col])
@@ -392,7 +415,7 @@
         fwd[u] = out.reshape(fwd.shape[1:])
 
 
-def tile_products(meta, tiles, cols, rows):
+def tile_products(meta, tiles, scales, cols, rows):
     plane, his, tile, _ = tiles.shape
     blocks, width = rows.shape[1], rows.shape[3]
     span = cols.shape[1]
@@ -404,6 +427,7 @@
             grid=(plane // step,),
             in_specs=[
                 pl.BlockSpec((step, his, tile, tile), lambda i, m: (i, 0, 0, 0)),
+                pl.BlockSpec((step,) + scales.shape[1:], lambda i, m: (i, 0, 0)),
                 pl.BlockSpec(cols.shape, lambda i, m: (0, 0, 0, 0)),
                 pl.BlockSpec((step, blocks, tile, width), lambda i, m: (i, 0, 0, 0)),
             ],
@@ -418,7 +442,7 @@
         ],
         compiler_params=pltpu.CompilerParams(vmem_limit_bytes=VMEM_LIMIT),
         name="tile_products",
-    )(meta, tiles, cols, rows)
+    )(meta, tiles, scales, cols, rows)
 
 
 CHUNK = 64
@@ -809,21 +833,39 @@
     return jnp.concatenate(out, axis=0)
 
 
-def basis_kernel(scale, gram, product, basis):
+def eliminated(gram, scale, inverse):
+    h = gram.shape[0] // 2
+    g21 = gram[h:, :h] * scale
+    w11 = inverse_factor(gram[:h, :h] * scale)
+    l21 = dot_high(g21, w11, ((1,), (1,)))
+    w22 = inverse_factor(gram[h:, h:] * scale - dot_high(l21, l21, ((1,), (1,))))
+    inverse[:h, :h] = w11
+    inverse[:h, h:] = jnp.zeros((h, h), jnp.float32)
+    inverse[h:, :h] = -dot_high(w22, dot_high(l21, w11, ((1,), (0,))), ((1,), (0,)))
+    inverse[h:, h:] = w22
+
+
+def basis_kernel(scale, gram, product, basis, inverse):
     n = gram.shape[0]
-    h = n // 2
-    g11 = gram[:h, :h] * scale
-    g21 = gram[h:, :h] * scale
-    g22 = gram[h:, h:] * scale
-    w11 = inverse_factor(g11)
-    l21 = dot_high(g21, w11, ((1,), (1,)))
-    w22 = inverse_factor(g22 - dot_high(l21, l21, ((1,), (1,))))
-    w21 = -dot_high(w22, dot_high(l21, w11, ((1,), (0,))), ((1,), (0,)))
-    first = product[:, :h]
-    basis[:, :h] = dot_high(first, w11, ((1,), (1,)))
-    basis[:, h:] = dot_high(first, w21, ((1,), (1,))) + dot_high(
-        product[:, h:], w22, ((1,), (1,))
-    )
+    line = lax.broadcasted_iota(jnp.int32, (n, n), 0)
+    lane = lax.broadcasted_iota(jnp.int32, (n, n), 1)
+    one = (line == lane).astype(jnp.float32)
+    weight = jnp.where(line > lane, 1.0, 0.5 * one)
+    g = gram[...] * scale
+    d_line = lax.rsqrt(jnp.sum(g * one, axis=1, keepdims=True))
+    d_lane = lax.rsqrt(jnp.sum(g * one, axis=0, keepdims=True))
+    w = (one - weight * (g * d_line * d_lane - one)) * d_lane
+    for turn in range(2):
+        off = dot_high(dot_high(w, g, ((1,), (0,))), w, ((1,), (1,))) - one
+        w = w - dot_high(weight * off, w, ((1,), (0,)))
+    inverse[...] = w
+    settled = jnp.sum(off * off) < 1e-6
+
+    @pl.when(jnp.logical_not(settled))
+    def _():
+        eliminated(gram, scale, inverse)
+
+    basis[...] = dot_high(product[...], inverse[...], ((1,), (1,)))
 
 
 def new_basis(gram, product, nodes):
@@ -833,6 +875,7 @@
         out_shape=jax.ShapeDtypeStruct(product.shape, jnp.float32),
         in_specs=[vmem, vmem],
         out_specs=vmem,
+        scratch_shapes=[pltpu.VMEM(gram.shape, jnp.float32)],
         compiler_params=pltpu.CompilerParams(vmem_limit_bytes=VMEM_LIMIT),
         name="new_basis",
     )(gram, product)
@@ -848,17 +891,12 @@
     nodes = panel.shape[0] * nz * plane
     his = nz // group
     own = panel.reshape(blocks, tile, width)
-    here, meta, cols, rows = bring(
-        own,
-        jnp.pad(lists, ((0, 8 - 3), (0, 128 - lists.shape[1] % 128))),
-        tiles.reshape(his, group * nx, tile, tile),
-    )
-    place = (lax.axis_index("y") * nc + lax.axis_index("core")) * nx + lax.axis_index("x")
-    meta = meta[:, :3, : lists.shape[1]].reshape(plane, 3, his, group * nx)
-    meta = lax.dynamic_index_in_dim(meta, place, 3, keepdims=False)
-    meta = meta.transpose(1, 0, 2).reshape(3, plane * his)
+    entries = lists.reshape(3, his, group, nx).transpose(3, 2, 1, 0).reshape(plane, 1, 3 * his)
+    entries = jnp.pad(entries.astype(jnp.float32), ((0, 0), (his, 7 - his), (0, 128 - 3 * his)))
+    here, meta, cols, rows = bring(own, entries, tiles.reshape(his, group * nx, tile, tile))
     rows = rows.reshape(plane, blocks, tile, width)
-    fwd, bwd = tile_products(meta, here, cols, rows)
+    picks = meta[:, his, : 3 * his].astype(jnp.int32).reshape(plane * his, 3).T
+    fwd, bwd = tile_products(picks, here, meta, cols, rows)
     product, gram = device_sums(
         fwd.reshape(plane, blocks * tile, width), bwd.reshape(his, group * blocks * tile, width)
     )

time: 260 us -> 248 us (0.954)
  Pallas kernels: 256 us -> 244 us
    pallas_call x1, Pallas kernels: 98 us -> 78.7 us  [bring(): pl.pallas_call(functools.partial(bring_kernel, sizes), out_shape=[jax.Sha...]
    pallas_call x1, Pallas kernels: 120 us -> 124 us  [device_sums(): pl.pallas_call(functools.partial(sums_kernel, sizes), out_shape=[jax.Shap...]
    pallas_call x1, Pallas kernels: 24.5 us -> 27.8 us  [new_basis(): pl.pallas_call(functools.partial(basis_kernel, 1.0 / nodes), out_shape=ja...]
where the time goes in v5:
time: 248 us; the launch traced here: 247 us
  Pallas kernels  244 us (98%)
    pallas_call x1, Pallas kernels, device_sums(): pl.pallas_call(functools.partial(sums_kernel, sizes), out_shape=[jax.Shap...  124 us
    pallas_call x1, Pallas kernels, bring(): pl.pallas_call(functools.partial(bring_kernel, sizes), out_shape=[jax.Sha...  78.7 us
    pallas_call x1, Pallas kernels, new_basis(): pl.pallas_call(functools.partial(basis_kernel, 1.0 / nodes), out_shape=ja...  27.8 us
    pallas_call x1, Pallas kernels, tile_products(): pl.pallas_call(functools.partial(tiles_kernel, his, blocks, span, step),...  13.1 us

profile of v5, /device:TPU:1, one launch (start us, length us, event | category | flops | bytes accessed | tf_op | source)
XLA Modules:
  0.0 247.5 jit_solution(16946855272713631236)
XLA Ops:
  0.0 0.7 convert_element_type.29
  0.7 0.1 convert_element_type.30
  0.8 0.1 copy.5
  0.9 0.1 convert_element_type.32
  1.0 0.1 copy.6
  1.1 0.7 pad.4.lists
  1.7 78.7 %bring.1 = (s16[32,2,128,128]{3,2,1,0:T(8,128)(2,1)}, f32[32,8,128]{2,1,0:T(8,128)}, bf16[2,16,128,256]{3,2,1,0:T(8,128)(2,1)}, bf16[4,4,2,2,128,256]{5,4,3,2,1,0:T(8,128)(2,1)}) custom-call(bf16[2,128,256]{2,1,0:T(8,128)(2,1)} %bitcast.13, f32[32,8,128]{2,1,0:T(8,128)} %pad.4.lists, f32[2,32,128,128]{3,2,1,0:T(8,128)} %bitcast.12), custom_call_target="tpu_custom_call" | custom-call | tf_op jit(solution)/shard_map/bring/pallas_call | solution.py:340
  80.4 1.0 convert_reduce_fusion
  81.4 0.1 convert_element_type.34
  81.5 0.7 copy.7
  82.1 13.1 %tile_products.1 = (f32[32,2,128,256]{3,2,1,0:T(8,128)}, f32[2,16,128,256]{3,2,1,0:T(8,128)}) custom-call(s32[3,64]{1,0:T(4,128)} %bitcast.15, s16[32,2,128,128]{3,2,1,0:T(8,128)(2,1)} %get-tuple-element.14.tiles, f32[32,8,128]{2,1,0:T(8,128)} %get-tuple-element.13.scales, bf16[2,16,128,256]{3,2,1,0:T(8,128)(2,1)} %get-tuple-element.15.cols, ...), custom_call_target="tpu_custom_call" | custom-call | tf_op jit(solution)/shard_map/tile_products/pallas_call | solution.py:423
  95.2 124.5 %device_sums.1 = (f32[256,256]{1,0:T(8,128)}, f32[256,256]{1,0:T(8,128)}) custom-call(f32[16,2,256,256]{3,2,1,0:T(8,128)} %bitcast.9, f32[2,32,64,256]{3,2,1,0:T(8,128)} %bitcast.10), custom_call_target="tpu_custom_call" | custom-call | tf_op jit(solution)/shard_map/device_sums/pallas_call | solution.py:765
  219.7 27.8 %new_basis.1 = f32[256,256]{1,0:T(8,128)} custom-call(f32[256,256]{1,0:T(8,128)} %get-tuple-element.19.gram, f32[256,256]{1,0:T(8,128)} %get-tuple-element.20.product), custom_call_target="tpu_custom_call" | custom-call | tf_op jit(solution)/shard_map/new_basis/pallas_call | solution.py:873

commit v6 on v5

--- a/solution.py
+++ b/solution.py
@@ -24,7 +24,6 @@
 
 
 CODE_TOP = 32767.0
-PASS = 3
 
 
 def bring_kernel(
@@ -39,15 +38,16 @@
     stage,
     coded,
     message,
+    passing,
     local_sem,
     tile_sent,
     tile_came,
     list_sent,
     list_came,
-    gather_sent,
-    gather_came,
-    chain_sent,
-    chain_came,
+    hold_sent,
+    hold_came,
+    ring_sent,
+    ring_came,
     first_sent,
     first_came,
     second_sent,
@@ -63,7 +63,6 @@
     g = y * nc + c
     me = x * group + g
     blocks = panel.shape[0]
-    chunks = cols.shape[1]
 
     def member(p):
         return (z, x, p // nc, lax.rem(p, nc))
@@ -99,38 +98,63 @@
     for device in (above, below):
         pl.semaphore_signal(barrier, inc=1, device_id=device, device_id_type=MESH)
 
-    holder = lax.rem(z, group)
-    his = z // group
     local = [
         pltpu.make_async_copy(panel, rows.at[x, y, c], local_sem.at[0]),
         pltpu.make_async_copy(coded.at[me], here.at[me], local_sem.at[1]),
         pltpu.make_async_copy(message.at[me], meta.at[me], local_sem.at[2]),
     ]
-    load = pltpu.make_async_copy(tiles, stage, local_sem.at[4])
+    load = pltpu.make_async_copy(tiles, stage, local_sem.at[3])
     load.start()
-    to_cols = pltpu.make_async_copy(
-        panel, cols.at[his, pl.ds(g * blocks, blocks)], local_sem.at[3]
-    )
     local[0].start()
 
-    @pl.when(holder == g)
-    def _():
-        to_cols.start()
-
     pl.semaphore_wait(barrier, plane - 1 + 2)
 
-    def gather(p):
+    def ring_copy(way, k, q, device):
+        source = panel if k == 1 else passing.at[q]
+        return remote(source, passing.at[q], ring_sent.at[way, k], ring_came.at[way, k], device)
+
+    def to_holder(k, q, source, of):
         return remote(
-            panel,
-            cols.at[his, pl.ds(p * blocks, blocks)],
-            gather_sent.at[0],
-            gather_came.at[p],
-            member(holder),
-        )
-
-    @pl.when(holder != g)
-    def _():
-        gather(g).start()
+            source,
+            cols.at[q // group, pl.ds(of * blocks, blocks)],
+            hold_sent.at[k],
+            hold_came.at[q // group, of],
+            member(lax.rem(q, group)),
+        )
+
+    def keep_block(k, q, source):
+        return pltpu.make_async_copy(
+            source, cols.at[q // group, pl.ds(g * blocks, blocks)], hold_sent.at[k]
+        )
+
+    def hand_over(k, q, source):
+        @pl.when(lax.rem(q, group) == g)
+        def _():
+            keep_block(k, q, source).start()
+
+        @pl.when(lax.rem(q, group) != g)
+        def _():
+            to_holder(k, q, source, g).start()
+
+    def at_ring(k):
+        return lax.rem(z + k + nz, nz)
+
+    ring_copy(0, 1, z, above).start()
+    ring_copy(1, 1, z, below).start()
+    hand_over(0, z, panel)
+
+    def ring_step(k):
+        q = at_ring(-k)
+        ring_copy(0, k, q, above).wait_recv()
+        if k < half:
+            ring_copy(0, k + 1, q, above).start()
+        hand_over(2 * k - 1, q, passing.at[q])
+        if k < half:
+            q = at_ring(k)
+            ring_copy(1, k, q, below).wait_recv()
+            if k < half - 1:
+                ring_copy(1, k + 1, q, below).start()
+            hand_over(2 * k, q, passing.at[q])
 
     def first_x(k, p, at):
         return remote(
@@ -177,63 +201,9 @@
     local[1].start()
     local[2].start()
 
-    d0 = lax.rem(g - z + nz, nz)
-    lower = jnp.logical_and(d0 >= 1, d0 <= half)
-    hu = jnp.where(lower, 0, 1)
-    hd = 1 - hu
-    du = jnp.where(lower, d0, lax.rem(d0 + half, nz))
-    dd = half - du
-    origin = du == half
-
-    def down(h, j):
-        return remote(
-            cols.at[h, j], cols.at[h, j], chain_sent.at[0, j], chain_came.at[0, j], below
-        )
-
-    def up(h, j):
-        return remote(
-            cols.at[h, j], cols.at[h, j], chain_sent.at[1, j], chain_came.at[1, j], above
-        )
-
-    def in_turn(j):
-        return lax.rem(g + j // blocks, group) * blocks + lax.rem(j, blocks)
-
-    @pl.when(origin)
-    def _():
-        to_cols.wait()
-        for m in range(group):
-            if m > 0:
-                gather(lax.rem(g + m, group)).wait_recv()
-            for b in range(blocks):
-                down(hd, in_turn(m * blocks + b)).start()
-                up(hd, in_turn(m * blocks + b)).start()
-
-    def step(i, carry):
-        j = i - PASS * (du - 1)
-
-        @pl.when(jnp.logical_and(j >= 0, j < chunks))
-        def _():
-            down(hu, in_turn(j)).wait_recv()
-
-            @pl.when(du < half)
-            def _():
-                down(hu, in_turn(j)).start()
-
-        ju = i - PASS * (dd - 1)
-
-        @pl.when(jnp.logical_and(jnp.logical_not(origin), jnp.logical_and(ju >= 0, ju < chunks)))
-        def _():
-            up(hd, in_turn(ju)).wait_recv()
-
-            @pl.when(dd < half - 1)
-            def _():
-                up(hd, in_turn(ju)).start()
-
-        return carry
-
-    steps = chunks + PASS * (half - 1)
-    cut = (steps // 3, (2 * steps) // 3)
-    lax.fori_loop(0, cut[0], step, 0)
+    cut = (1 + half // 4, 1 + (3 * half) // 4)
+    for k in range(1, cut[0]):
+        ring_step(k)
 
     def second_y(k, p, at):
         part = rows.at[:, at, c, 0]
@@ -256,7 +226,8 @@
     for k in range(1, nx):
         second_x(k, lax.rem(x + k, nx), x).start()
 
-    lax.fori_loop(cut[0], cut[1], step, 0)
+    for k in range(cut[0], cut[1]):
+        ring_step(k)
 
     def core_y(p, of):
         part = rows.at[:, p, of, 0]
@@ -277,7 +248,8 @@
         second_x(k, p, p).wait_recv()
         core_x(p, c).start()
 
-    lax.fori_loop(cut[1], steps, step, 0)
+    for k in range(cut[1], half + 1):
+        ring_step(k)
 
     def finish(k, carry):
         p, device = plane_peer(k)
@@ -303,27 +275,26 @@
         first_y(k, p, y).wait_send()
         second_y(k, p, y).wait_send()
 
-    @pl.when(holder != g)
-    def _():
-        gather(g).wait_send()
-
-    def drain(j, carry):
-        @pl.when(origin)
-        def _():
-            down(hd, j).wait_send()
-            up(hd, j).wait_send()
-
-        @pl.when(du < half)
-        def _():
-            down(hu, j).wait_send()
-
-        @pl.when(jnp.logical_and(jnp.logical_not(origin), dd < half - 1))
-        def _():
-            up(hd, j).wait_send()
-
-        return carry
-
-    lax.fori_loop(0, chunks, drain, 0)
+    for k in range(1, half + 1):
+        ring_copy(0, k, at_ring(1 - k), above).wait_send()
+        if k < half:
+            ring_copy(1, k, at_ring(k - 1), below).wait_send()
+    for k in range(nz):
+        q = z if k == 0 else at_ring(-(k + 1) // 2 if k % 2 else k // 2)
+        source = panel if k == 0 else passing.at[q]
+
+        @pl.when(lax.rem(q, group) == g)
+        def _(k=k, q=q, source=source):
+            keep_block(k, q, source).wait()
+
+        @pl.when(lax.rem(q, group) != g)
+        def _(k=k, q=q, source=source):
+            to_holder(k, q, source, g).wait_send()
+
+    for h in range(nz // group):
+        for m in range(1, group):
+            of = lax.rem(g + m, group)
+            to_holder(0, h * group + g, panel, of).wait_recv()
 
 
 def bring(panel, lists, tiles):
@@ -351,15 +322,16 @@
             pltpu.VMEM(tiles.shape, jnp.float32),
             pltpu.VMEM((plane, his, tile, tile), jnp.int16),
             pltpu.VMEM(lists.shape, jnp.float32),
-            dma((5,)),
+            pltpu.VMEM((nz, blocks, tile, width), jnp.bfloat16),
+            dma((4,)),
             dma((plane,)),
             dma((plane,)),
             dma((plane,)),
             dma((plane,)),
-            dma((1,)),
-            dma((group,)),
-            dma((2, span)),
-            dma((2, span)),
+            dma((nz,)),
+            dma((his, group)),
+            dma((2, nz // 2 + 1)),
+            dma((2, nz // 2 + 1)),
             dma((2, most)),
             dma((2, most)),
             dma((2, most)),
@@ -460,6 +432,8 @@
     from_core,
     from_x,
     from_y,
+    end_x,
+    end_y,
     from_below,
     from_above,
     last,
@@ -521,14 +495,14 @@
     lax.fori_loop(1, plane, greet(plane_peer), 0)
     lax.fori_loop(1, nz, greet(ring_peer), 0)
     load_held = pltpu.make_async_copy(bwd, held, local_sem.at[0])
-    load_keep = pltpu.make_async_copy(fwd.at[:, c], keep, local_sem.at[1])
+    load_keep = pltpu.make_async_copy(fwd.at[:, :, c], keep, local_sem.at[1])
     load_held.start()
     load_keep.start()
     pl.semaphore_wait(barrier, plane - 1 + nz - 1)
 
     other = (z, x, y, nc - 1 - c)
     core_copy = remote(
-        fwd.at[:, nc - 1 - c], from_core, plane_sent.at[0, 0], plane_came.at[0, 0], other
+        fwd.at[:, :, nc - 1 - c], from_core, plane_sent.at[0, 0], plane_came.at[0, 0], other
     )
     core_copy.start()
 
@@ -603,73 +577,109 @@
         return carry
 
     steps = chunks + SKEW * half
-    cut = (steps // 5, (3 * steps) // 4)
+    cut = (steps // 6, (3 * steps) // 5)
     lax.fori_loop(0, cut[0], step, 0)
 
     load_keep.wait()
     core_copy.wait()
+    rows = keep.shape[2]
+    top, low = pl.ds(0, rows // 2), pl.ds(rows // 2, rows // 2)
+
+    def add_core(i, carry):
+        at = (i // ny, lax.rem(i, ny))
+        keep[at] += from_core[at]
+        return carry
+
+    lax.fori_loop(0, nx * ny, add_core, 0)
 
     def x_copy(k):
         p = lax.rem(x + k, nx)
         return remote(
-            keep.at[pl.ds(p * ny, ny)],
+            keep.at[p, :, top],
             from_x.at[x],
             plane_sent.at[1, k],
             plane_came.at[1, x],
             (z, p, y, c),
         )
 
+    def y_copy(k):
+        p = lax.rem(y + k, ny)
+        return remote(
+            keep.at[:, p, low],
+            from_y.at[y],
+            plane_sent.at[2, k],
+            plane_came.at[2, y],
+            (z, x, p, c),
+        )
+
+    for k in range(1, max(nx, ny)):
+        if k < nx:
+            x_copy(k).start()
+        if k < ny:
+            y_copy(k).start()
+
+    lax.fori_loop(cut[0], cut[1], step, 0)
+
     def x_source(k):
         p = lax.rem(x + k, nx)
         return p, remote(
             from_x.at[p], from_x.at[p], plane_sent.at[1, k], plane_came.at[1, p], (z, p, y, c)
         )
 
-    for k in range(1, nx + 1):
-        p = lax.rem(x + k, nx)
-
-        def add_core(i, carry, p=p):
-            keep[p * ny + i] += from_core[p * ny + i]
-            return carry
-
-        lax.fori_loop(0, ny, add_core, 0)
-        if k < nx:
-            x_copy(k).start()
-
-    lax.fori_loop(cut[0], cut[1], step, 0)
+    def y_source(k):
+        p = lax.rem(y + k, ny)
+        return p, remote(
+            from_y.at[p], from_y.at[p], plane_sent.at[2, k], plane_came.at[2, p], (z, x, p, c)
+        )
 
     for k in range(1, nx):
         p, copy = x_source(k)
         copy.wait_recv()
-
-        def add_x(i, carry, p=p):
-            keep[x * ny + i] += from_x[p, i]
-            return carry
-
-        lax.fori_loop(0, ny, add_x, 0)
-
-    def y_copy(k):
+        keep[x, :, top] += from_x[p]
+    for k in range(1, ny):
+        p, copy = y_source(k)
+        copy.wait_recv()
+        keep[:, y, low] += from_y[p]
+
+    def last_y(k, at):
         p = lax.rem(y + k, ny)
         return remote(
-            keep.at[x * ny + p],
-            from_y.at[y],
-            plane_sent.at[2, k],
-            plane_came.at[2, y],
+            keep.at[x, p, top],
+            end_y.at[at],
+            plane_sent.at[3, k],
+            plane_came.at[3, at],
             (z, x, p, c),
         )
 
-    for k in range(1, ny):
-        y_copy(k).start()
+    def last_x(k, at):
+        p = lax.rem(x + k, nx)
+        return remote(
+            keep.at[p, y, low],
+            end_x.at[at],
+            plane_sent.at[4, k],
+            plane_came.at[4, at],
+            (z, p, y, c),
+        )
+
+    for k in range(1, max(nx, ny)):
+        if k < ny:
+            last_y(k, y).start()
+        if k < nx:
+            last_x(k, x).start()
 
     lax.fori_loop(cut[1], steps, step, 0)
 
-    total = keep[x * ny + y]
+    upper = keep[x, y, top]
     for k in range(1, ny):
         p = lax.rem(y + k, ny)
-        remote(
-            from_y.at[p], from_y.at[p], plane_sent.at[2, k], plane_came.at[2, p], (z, x, p, c)
-        ).wait_recv()
-        total = total + from_y[p]
+        last_y(k, p).wait_recv()
+        upper = upper + end_y[p]
+    lower_rows = keep[x, y, low]
+    for k in range(1, nx):
+        p = lax.rem(x + k, nx)
+        last_x(k, p).wait_recv()
+        lower_rows = lower_rows + end_x[p]
+    total = jnp.concatenate([upper, lower_rows], axis=0)
     holder = lax.rem(z, group)
 
     @pl.when(holder != g)
@@ -725,8 +735,10 @@
 
     for k in range(1, nx):
         x_copy(k).wait_send()
+        last_x(k, x).wait_send()
     for k in range(1, ny):
         y_copy(k).wait_send()
+        last_y(k, y).wait_send()
 
     def drain(j, carry):
         up(j).wait_send()
@@ -753,7 +765,7 @@
     strip = width // plane
     most = max(plane, nz)
     chunks = group * rows // CHUNK
-    fwd = fwd.reshape(nx * ny, nc, rows, width)
+    fwd = fwd.reshape(nx, ny, nc, rows, width)
     bwd = bwd.reshape(2, chunks, CHUNK, width)
     vmem = pl.BlockSpec(memory_space=pltpu.VMEM)
     anywhere = pl.BlockSpec(memory_space=pl.ANY)
@@ -772,10 +784,12 @@
         out_specs=[vmem, vmem],
         scratch_shapes=[
             buffer(2, chunks, CHUNK, width),
-            buffer(nx * ny, rows, width),
-            buffer(nx * ny, rows, width),
             buffer(nx, ny, rows, width),
-            buffer(ny, rows, width),
+            buffer(nx, ny, rows, width),
+            buffer(nx, ny, rows // 2, width),
+            buffer(ny, nx, rows // 2, width),
+            buffer(nx, rows // 2, width),
+            buffer(ny, rows // 2, width),
             buffer(chunks, CHUNK, width),
             buffer(chunks, CHUNK, width),
             buffer(rows // CHUNK, CHUNK, width),
@@ -788,8 +802,8 @@
             dma((2, chunks)),
             dma((chunks,)),
             dma((rows // CHUNK,)),
-            dma((3, max(nx, ny))),
-            dma((3, max(nx, ny))),
+            dma((5, max(nx, ny))),
+            dma((5, max(nx, ny))),
             dma((3, most)),
             dma((3, most)),
         ],

time: 248 us -> 237 us (0.956)
  Pallas kernels: 244 us -> 233 us
    pallas_call x1, Pallas kernels: 124 us -> 117 us  [device_sums(): pl.pallas_call(functools.partial(sums_kernel, sizes), out_shape=[jax.Shap...]
    pallas_call x1, Pallas kernels: 78.7 us -> 75.3 us  [bring(): pl.pallas_call(functools.partial(bring_kernel, sizes), out_shape=[jax.Sha...]
where the time goes in v6:
time: 237 us; the launch traced here: 236 us
  Pallas kernels  233 us (98%)
    pallas_call x1, Pallas kernels, device_sums(): pl.pallas_call(functools.partial(sums_kernel, sizes), out_shape=[jax.Shap...  117 us
    pallas_call x1, Pallas kernels, bring(): pl.pallas_call(functools.partial(bring_kernel, sizes), out_shape=[jax.Sha...  75.3 us
    pallas_call x1, Pallas kernels, new_basis(): pl.pallas_call(functools.partial(basis_kernel, 1.0 / nodes), out_shape=ja...  27.8 us
    pallas_call x1, Pallas kernels, tile_products(): pl.pallas_call(functools.partial(tiles_kernel, his, blocks, span, step),...  13.1 us

profile of v6, /device:TPU:1, one launch (start us, length us, event | category | flops | bytes accessed | tf_op | source)
XLA Modules:
  0.0 236.3 jit_solution(10939353586885634554)
XLA Ops:
  0.0 0.7 convert_element_type.29
  0.7 0.1 convert_element_type.30
  0.8 0.1 copy.5
  0.9 0.1 convert_element_type.32
  1.0 0.1 copy.6
  1.1 0.7 pad.4.lists
  1.7 75.3 %bring.1 = (s16[32,2,128,128]{3,2,1,0:T(8,128)(2,1)}, f32[32,8,128]{2,1,0:T(8,128)}, bf16[2,16,128,256]{3,2,1,0:T(8,128)(2,1)}, bf16[4,4,2,2,128,256]{5,4,3,2,1,0:T(8,128)(2,1)}) custom-call(bf16[2,128,256]{2,1,0:T(8,128)(2,1)} %bitcast.13, f32[32,8,128]{2,1,0:T(8,128)} %pad.4.lists, f32[2,32,128,128]{3,2,1,0:T(8,128)} %bitcast.12), custom_call_target="tpu_custom_call" | custom-call | tf_op jit(solution)/shard_map/bring/pallas_call | solution.py:311
  77.0 1.0 convert_reduce_fusion
  78.0 0.1 convert_element_type.34
  78.1 0.7 copy.7
  78.7 13.1 %tile_products.1 = (f32[32,2,128,256]{3,2,1,0:T(8,128)}, f32[2,16,128,256]{3,2,1,0:T(8,128)}) custom-call(s32[3,64]{1,0:T(4,128)} %bitcast.15, s16[32,2,128,128]{3,2,1,0:T(8,128)(2,1)} %get-tuple-element.14.tiles, f32[32,8,128]{2,1,0:T(8,128)} %get-tuple-element.13.scales, bf16[2,16,128,256]{3,2,1,0:T(8,128)(2,1)} %get-tuple-element.15.cols, ...), custom_call_target="tpu_custom_call" | custom-call | tf_op jit(solution)/shard_map/tile_products/pallas_call | solution.py:395
  91.8 116.7 %device_sums.1 = (f32[256,256]{1,0:T(8,128)}, f32[256,256]{1,0:T(8,128)}) custom-call(f32[4,4,2,256,256]{4,3,2,1,0:T(8,128)} %bitcast.9, f32[2,32,64,256]{3,2,1,0:T(8,128)} %bitcast.10), custom_call_target="tpu_custom_call" | custom-call | tf_op jit(solution)/shard_map/device_sums/pallas_call | solution.py:777
  208.5 27.8 %new_basis.1 = f32[256,256]{1,0:T(8,128)} custom-call(f32[256,256]{1,0:T(8,128)} %get-tuple-element.19.gram, f32[256,256]{1,0:T(8,128)} %get-tuple-element.20.product), custom_call_target="tpu_custom_call" | custom-call | tf_op jit(solution)/shard_map/new_basis/pallas_call | solution.py:887

commit v7 on v6

--- a/solution.py
+++ b/solution.py
@@ -381,9 +381,10 @@
         )
         right = jnp.concatenate(panels, axis=0)
         high, low = split2(left)
-        out = jnp.dot(high, right, preferred_element_type=jnp.float32) + jnp.dot(
-            low, right, preferred_element_type=jnp.float32
-        )
+        both = jnp.dot(
+            jnp.concatenate([high, low], axis=0), right, preferred_element_type=jnp.float32
+        )
+        out = both[: left.shape[0]] + both[left.shape[0] :]
         fwd[u] = out.reshape(fwd.shape[1:])
 
 
@@ -709,30 +710,38 @@
 
         def finish(k, carry):
             p, device = peer(k)
-            copy(k, p, device).wait_send()
             remote(
                 target_of(p), target_of(p), sent.at[stage, k], came.at[stage, p], device
             ).wait_recv()
             return carry
 
+        def left(k, carry):
+            p, device = peer(k)
+            copy(k, p, device).wait_send()
+            return carry
+
         lax.fori_loop(1, count, start, 0)
         lax.fori_loop(1, count, finish, 0)
-
-    exchange(plane, plane_peer, 0, me, lambda p: part.at[rows_of(p)], lambda p: got.at[p])
+        return lambda: lax.fori_loop(1, count, left, 0)
+
+    left_first = exchange(plane, plane_peer, 0, me, lambda p: part.at[rows_of(p)], lambda p: got.at[p])
     strip_sum = part[rows_of(me)]
     for k in range(1, plane):
         strip_sum = strip_sum + got[lax.rem(me + k, plane)]
     ring[z] = strip_sum
-    exchange(nz, ring_peer, 1, z, lambda p: ring.at[z], lambda p: ring.at[p])
+    left_ring = exchange(nz, ring_peer, 1, z, lambda p: ring.at[z], lambda p: ring.at[p])
     strip_sum = ring[0]
     for k in range(1, nz):
         strip_sum = strip_sum + ring[k]
     whole[rows_of(me)] = strip_sum
-    exchange(
+    left_last = exchange(
         plane, plane_peer, 2, me, lambda p: whole.at[rows_of(me)], lambda p: whole.at[rows_of(p)]
     )
     gram[...] = whole[...]
 
+    left_first()
+    left_ring()
+    left_last()
     for k in range(1, nx):
         x_copy(k).wait_send()
         last_x(k, x).wait_send()

time: 237 us -> 237 us (level)
  no operation moved by 1% of the time
where the time goes in v7:
time: 237 us
  Pallas kernels  233 us (98%)
    pallas_call x1, Pallas kernels, device_sums(): pl.pallas_call(functools.partial(sums_kernel, sizes), out_shape=[jax.Shap...  117 us
    pallas_call x1, Pallas kernels, bring(): pl.pallas_call(functools.partial(bring_kernel, sizes), out_shape=[jax.Sha...  75.3 us
    pallas_call x1, Pallas kernels, new_basis(): pl.pallas_call(functools.partial(basis_kernel, 1.0 / nodes), out_shape=ja...  27.8 us
    pallas_call x1, Pallas kernels, tile_products(): pl.pallas_call(functools.partial(tiles_kernel, his, blocks, span, step),...  13.1 us

profile of v7, /device:TPU:1, one launch (start us, length us, event | category | flops | bytes accessed | tf_op | source)
XLA Modules:
  0.0 236.6 jit_solution(3926733901444362808)
XLA Ops:
  0.0 0.7 convert_element_type.29
  0.7 0.1 convert_element_type.30
  0.8 0.1 copy.5
  0.9 0.1 convert_element_type.32
  1.0 0.1 copy.6
  1.1 0.7 pad.4.lists
  1.7 75.3 %bring.1 = (s16[32,2,128,128]{3,2,1,0:T(8,128)(2,1)}, f32[32,8,128]{2,1,0:T(8,128)}, bf16[2,16,128,256]{3,2,1,0:T(8,128)(2,1)}, bf16[4,4,2,2,128,256]{5,4,3,2,1,0:T(8,128)(2,1)}) custom-call(bf16[2,128,256]{2,1,0:T(8,128)(2,1)} %bitcast.13, f32[32,8,128]{2,1,0:T(8,128)} %pad.4.lists, f32[2,32,128,128]{3,2,1,0:T(8,128)} %bitcast.12), custom_call_target="tpu_custom_call" | custom-call | tf_op jit(solution)/shard_map/bring/pallas_call | solution.py:311
  77.0 1.0 convert_reduce_fusion
  78.0 0.1 convert_element_type.34
  78.1 0.7 copy.7
  78.7 13.1 %tile_products.1 = (f32[32,2,128,256]{3,2,1,0:T(8,128)}, f32[2,16,128,256]{3,2,1,0:T(8,128)}) custom-call(s32[3,64]{1,0:T(4,128)} %bitcast.15, s16[32,2,128,128]{3,2,1,0:T(8,128)(2,1)} %get-tuple-element.14.tiles, f32[32,8,128]{2,1,0:T(8,128)} %get-tuple-element.13.scales, bf16[2,16,128,256]{3,2,1,0:T(8,128)(2,1)} %get-tuple-element.15.cols, ...), custom_call_target="tpu_custom_call" | custom-call | tf_op jit(solution)/shard_map/tile_products/pallas_call | solution.py:396
  91.8 117.1 %device_sums.1 = (f32[256,256]{1,0:T(8,128)}, f32[256,256]{1,0:T(8,128)}) custom-call(f32[4,4,2,256,256]{4,3,2,1,0:T(8,128)} %bitcast.9, f32[2,32,64,256]{3,2,1,0:T(8,128)} %bitcast.10), custom_call_target="tpu_custom_call" | custom-call | tf_op jit(solution)/shard_map/device_sums/pallas_call | solution.py:786
  208.9 27.8 %new_basis.1 = f32[256,256]{1,0:T(8,128)} custom-call(f32[256,256]{1,0:T(8,128)} %get-tuple-element.19.gram, f32[256,256]{1,0:T(8,128)} %get-tuple-element.20.product), custom_call_target="tpu_custom_call" | custom-call | tf_op jit(solution)/shard_map/new_basis/pallas_call | solution.py:896
